TPU v7x, 256 devices: a whole 4x4x8 slice. The times are simulated.
256 devices in a mesh: head: 4 (over y), ctx: 64 (over x, z, core).
Axes of the slice: x: 4, y: 4, z: 8, core: 2. Of those that a mesh axis runs over, the one named last changes fastest.
Arguments:
- query: bfloat16 [64, 512, 4096], P('ctx', 'head'), may hold values from -6 to 6
- keys: bfloat16 [64, 512, 4096], P('ctx', 'head'), may hold values from -6 to 6
- values: bfloat16 [64, 512, 4096], P('ctx', 'head'), may hold values from -6 to 6
- grad_out: bfloat16 [64, 512, 4096], P('ctx', 'head'), may hold values from -6 to 6
Outputs:
- grad_q: bfloat16 [64, 512, 4096], P('ctx', None, 'head')
- grad_k: bfloat16 [64, 512, 4096], P('ctx', None, 'head')
- grad_v: bfloat16 [64, 512, 4096], P('ctx', None, 'head')
All inputs are finite; a program needn't handle non-finite values.
Results may differ from a plain program's by a relative error of at most 0.0049.
Values may be sent and summed in bfloat16 or wider, within the bound.
A program may use at most 192 MiB of HBM per device.

v0:
```python
import jax
import jax.numpy as jnp
from jax import lax
from jax.sharding import PartitionSpec as P

HD = 128
BLOCK = 512


def shifted(value, axis, steps):
    count = lax.axis_size(axis)
    leading, last = (max(0, -steps), min(count, count - steps))
    return lax.ppermute(value, axis, [(source, source + steps) for source in range(leading, last)])


def earlier_total(state):
    total = state
    distance = 1
    while distance < lax.axis_size("ctx"):
        total = total + shifted(total, "ctx", distance)
        distance = distance * 2
    return total


def later_total(state):
    total = state
    distance = 1
    while distance < lax.axis_size("ctx"):
        total = total + shifted(total, "ctx", -distance)
        distance = distance * 2
    return total


def shards(query, keys, values, grad_out):
    query_part, keys_part, values_part, grads_part = (
        lax.all_to_all(query, "head", split_axis=2, concat_axis=1, tiled=True),
        lax.all_to_all(keys, "head", split_axis=2, concat_axis=1, tiled=True),
        lax.all_to_all(values, "head", split_axis=2, concat_axis=1, tiled=True),
        lax.all_to_all(grad_out, "head", split_axis=2, concat_axis=1, tiled=True),
    )
    row_count = keys_part.shape[1]
    full_width = keys_part.shape[2]
    head_count = full_width // HD
    count = row_count // BLOCK
    length = row_count * lax.axis_size("ctx")
    factor = (HD * length) ** (-0.5)

    def split_heads(x):
        return x.reshape(count, BLOCK, head_count, HD).transpose(0, 2, 1, 3)

    query_blocks = split_heads(query_part)
    keys_blocks = split_heads(keys_part)
    values_blocks = split_heads(values_part)
    grads_blocks = split_heads(grads_part)
    key_own = jnp.einsum(
        "nhca,nhcb->nhab", keys_blocks, values_blocks, preferred_element_type=jnp.float32
    )
    query_own = jnp.einsum(
        "nhca,nhcb->nhab", query_blocks, grads_blocks, preferred_element_type=jnp.float32
    )
    key_device = jnp.sum(key_own, 0)
    query_device = jnp.sum(query_own, 0)
    key_prior = earlier_total(key_device) - key_device
    query_later = later_total(query_device) - query_device
    key_states = key_prior[None] + (jnp.cumsum(key_own, 0) - key_own)
    query_states = query_later[None] + (query_device[None] - jnp.cumsum(query_own, 0))
    key_rounded = key_states.astype(jnp.bfloat16)
    query_rounded = query_states.astype(jnp.bfloat16)
    causal = jnp.tril(jnp.ones((BLOCK, BLOCK), jnp.bool_))
    out_scores = (
        jnp.einsum(
            "nhpd,nhtd->nhpt", grads_blocks, values_blocks, preferred_element_type=jnp.float32
        )
        * factor
    )
    out_scores = jnp.where(causal[None, None], out_scores, 0.0).astype(jnp.bfloat16)
    key_scores = (
        jnp.einsum("nhpd,nhtd->nhpt", query_blocks, keys_blocks, preferred_element_type=jnp.float32)
        * factor
    )
    key_scores = jnp.where(causal[None, None], key_scores, 0.0).astype(jnp.bfloat16)
    grad_query = jnp.einsum(
        "nhpt,nhtd->nhpd", out_scores, keys_blocks, preferred_element_type=jnp.float32
    )
    grad_query = grad_query + factor * jnp.einsum(
        "nhpe,nhde->nhpd", grads_blocks, key_rounded, preferred_element_type=jnp.float32
    )
    grad_key = jnp.einsum(
        "nhpt,nhpd->nhtd", out_scores, query_blocks, preferred_element_type=jnp.float32
    )
    grad_key = grad_key + factor * jnp.einsum(
        "nhte,nhde->nhtd", values_blocks, query_rounded, preferred_element_type=jnp.float32
    )
    grad_value = jnp.einsum(
        "nhpt,nhpe->nhte", key_scores, grads_blocks, preferred_element_type=jnp.float32
    )
    grad_value = grad_value + factor * jnp.einsum(
        "nhtd,nhde->nhte", keys_blocks, query_rounded, preferred_element_type=jnp.float32
    )
    shape = (1, row_count, full_width)

    def merge_heads(x):
        return x.astype(jnp.bfloat16).transpose(0, 2, 1, 3).reshape(shape)

    return (merge_heads(grad_query), merge_heads(grad_key), merge_heads(grad_value))


def solution(mesh):
    in_specs = (
        P("ctx", "head", None),
        P("ctx", "head", None),
        P("ctx", "head", None),
        P("ctx", "head", None),
    )
    out_specs = (P("ctx", None, "head"), P("ctx", None, "head"), P("ctx", None, "head"))
    return jax.shard_map(shards, mesh=mesh, in_specs=in_specs, out_specs=out_specs, check_vma=False)
```

profile of v0, /device:TPU:40, one launch (start us, length us, event | category | flops | bytes accessed | tf_op | source)
XLA Modules:
  0.0 339.2 jit_solution(2826898758507407761)
XLA Ops:
  0.6 5.0 %copy.45 = bf16[1,128,4096]{1,0,2:T(2,128)(2,1)S(1)} copy(bf16[1,128,4096]{2,1,0:T(8,128)(2,1)} %param.7) | data formatting | bytes 2097152 | tf_op args[3]
  6.2 22.4 %reduce.1 = bf16[4096,128]{1,0:T(8,128)(2,1)S(1)} reduce(bf16[4096,1,128]{2,1,0:T(2,128)(2,1)S(1)} %bitcast.120, bf16[]{:T(256)} %broadcast.34), dimensions={1}, to_apply=%bitcast.98.reduce_sub_computation | reduce | bytes 2097154
  28.6 1.7 reshape.124
  30.2 4.9 %all-to-all-start = ((bf16[4,2,65536]{2,1,0:T(2,128)(2,1)}), bf16[4,2,65536]{2,1,0:T(2,128)(2,1)S(1)}, u32[]{:S(2)}, u32[]{:S(2)}) async-start(bf16[4,2,65536]{2,1,0:T(2,128)(2,1)} %reshape.124), calls=%async_computation | async-start | bytes 2097152 | tf_op jit(solution)/shard_map/all_to_all | solution.py:39
  35.2 5.0 %copy.53 = bf16[1,128,4096]{1,0,2:T(2,128)(2,1)S(1)} copy(bf16[1,128,4096]{2,1,0:T(8,128)(2,1)} %param.4) | data formatting | bytes 2097152 | tf_op args[0]
  40.2 23.4 %reduce.3 = bf16[4096,128]{1,0:T(8,128)(2,1)} reduce(bf16[4096,1,128]{2,1,0:T(2,128)(2,1)S(1)} %bitcast.122, bf16[]{:T(256)} %broadcast.34), dimensions={1}, to_apply=%bitcast.102.reduce_sub_computation | reduce | bytes 2097154
  63.5 3.5 %reshape.128 = bf16[4,2,65536]{2,1,0:T(2,128)(2,1)} reshape(bf16[4096,128]{1,0:T(8,128)(2,1)} %reduce.3) | data formatting | bytes 2097152
  67.0 4.8 %all-to-all-start.3 = ((bf16[4,2,65536]{2,1,0:T(2,128)(2,1)}), bf16[4,2,65536]{2,1,0:T(2,128)(2,1)}, u32[]{:S(2)}, u32[]{:S(2)}) async-start(bf16[4,2,65536]{2,1,0:T(2,128)(2,1)} %reshape.128), calls=%async_computation.3 | async-start | bytes 2097152 | tf_op jit(solution)/shard_map/all_to_all | solution.py:36
  71.8 5.0 %copy.51 = bf16[1,128,4096]{1,0,2:T(2,128)(2,1)S(1)} copy(bf16[1,128,4096]{2,1,0:T(8,128)(2,1)} %param.5) | data formatting | bytes 2097152 | tf_op args[1]
  76.9 23.4 %reduce.2 = bf16[4096,128]{1,0:T(8,128)(2,1)} reduce(bf16[4096,1,128]{2,1,0:T(2,128)(2,1)S(1)} %bitcast.123, bf16[]{:T(256)} %broadcast.34), dimensions={1}, to_apply=%bitcast.100.reduce_sub_computation | reduce | bytes 2097154
  100.2 3.5 %reshape.126 = bf16[4,2,65536]{2,1,0:T(2,128)(2,1)} reshape(bf16[4096,128]{1,0:T(8,128)(2,1)} %reduce.2) | data formatting | bytes 2097152
  103.7 4.8 %all-to-all-start.2 = ((bf16[4,2,65536]{2,1,0:T(2,128)(2,1)}), bf16[4,2,65536]{2,1,0:T(2,128)(2,1)}, u32[]{:S(2)}, u32[]{:S(2)}) async-start(bf16[4,2,65536]{2,1,0:T(2,128)(2,1)} %reshape.126), calls=%async_computation.2 | async-start | bytes 2097152 | tf_op jit(solution)/shard_map/all_to_all | solution.py:37
  108.5 5.0 %copy.48 = bf16[1,128,4096]{1,0,2:T(2,128)(2,1)S(1)} copy(bf16[1,128,4096]{2,1,0:T(8,128)(2,1)} %param.6) | data formatting | bytes 2097152 | tf_op args[2]
  113.5 23.4 %reduce = bf16[4096,128]{1,0:T(8,128)(2,1)} reduce(bf16[4096,1,128]{2,1,0:T(2,128)(2,1)S(1)} %bitcast.121, bf16[]{:T(256)} %broadcast.34), dimensions={1}, to_apply=%bitcast.96.reduce_sub_computation | reduce | bytes 2097154
  136.9 3.5 %reshape.122 = bf16[4,2,65536]{2,1,0:T(2,128)(2,1)} reshape(bf16[4096,128]{1,0:T(8,128)(2,1)} %reduce) | data formatting | bytes 2097152
  140.3 4.8 %all-to-all-start.1 = ((bf16[4,2,65536]{2,1,0:T(2,128)(2,1)}), bf16[4,2,65536]{2,1,0:T(2,128)(2,1)}, u32[]{:S(2)}, u32[]{:S(2)}) async-start(bf16[4,2,65536]{2,1,0:T(2,128)(2,1)} %reshape.122), calls=%async_computation.1 | async-start | bytes 2097152 | tf_op jit(solution)/shard_map/all_to_all | solution.py:38
  145.1 0.9 reshape.125
  147.1 2.6 reshape.129
  149.9 0.8 copy.54
  151.1 1.3 fusion.12
  152.4 1.9 collective-permute-start.6
  154.3 4.0 %reshape.127 = bf16[4096,1,128]{2,1,0:T(2,128)(2,1)} reshape(bf16[4,2,65536]{2,1,0:T(2,128)(2,1)} %all-to-all-done.2) | data formatting | bytes 2097152
  158.3 1.7 copy.72
  160.0 1.8 copy.52
  161.8 1.5 reshape.115
  163.3 4.0 %reshape.123 = bf16[4096,1,128]{2,1,0:T(2,128)(2,1)} reshape(bf16[4,2,65536]{2,1,0:T(2,128)(2,1)} %all-to-all-done.1) | data formatting | bytes 2097152
  167.2 2.7 copy.71
  169.9 2.3 copy.49
  172.2 1.5 copy.75
  174.2 2.4 collective-permute-start
  176.6 1.3 add.68
  177.9 2.8 collective-permute-start.7
  180.7 4.0 %collective-permute-done = f32[8,128,128]{2,1,0:T(8,128)S(1)} collective-permute-done((f32[8,128,128]{2,1,0:T(8,128)S(1)}, f32[8,128,128]{2,1,0:T(8,128)S(1)}, u32[]{:S(2)}, u32[]{:S(2)}) %collective-permute-start) | collective-permute-done | bytes 524320 | tf_op jit(solution)/shard_map/ppermute | solution.py:13
  184.8 3.8 %collective-permute-start.1 = (f32[8,128,128]{2,1,0:T(8,128)S(1)}, f32[8,128,128]{2,1,0:T(8,128)S(1)}, u32[]{:S(2)}, u32[]{:S(2)}) collective-permute-start(f32[8,128,128]{2,1,0:T(8,128)S(1)} %add.60), channel_id=1, source_target_pairs={{0,2},{1,3},{2,4},{3,5},{4,6},{5,7},{6,8},{7,9},{8,10},{9,11},{10,... | collective-permute-start | bytes 1572872 | tf_op jit(solution)/shard_map/ppermute | solution.py:13
  188.6 5.3 %collective-permute-done.7 = f32[8,128,128]{2,1,0:T(8,128)S(1)} collective-permute-done((f32[8,128,128]{2,1,0:T(8,128)S(1)}, f32[8,128,128]{2,1,0:T(8,128)S(1)}, u32[]{:S(2)}, u32[]{:S(2)}) %collective-permute-start.7) | collective-permute-done | bytes 524320 | tf_op jit(solution)/shard_map/ppermute | solution.py:13
  193.9 1.3 collective-permute-start.8
  195.2 4.8 %collective-permute-done.1 = f32[8,128,128]{2,1,0:T(8,128)S(1)} collective-permute-done((f32[8,128,128]{2,1,0:T(8,128)S(1)}, f32[8,128,128]{2,1,0:T(8,128)S(1)}, u32[]{:S(2)}, u32[]{:S(2)}) %collective-permute-start.1) | collective-permute-done | bytes 524320 | tf_op jit(solution)/shard_map/ppermute | solution.py:13
  200.1 6.4 %collective-permute-start.2 = (f32[8,128,128]{2,1,0:T(8,128)S(1)}, f32[8,128,128]{2,1,0:T(8,128)S(1)}, u32[]{:S(2)}, u32[]{:S(2)}) collective-permute-start(f32[8,128,128]{2,1,0:T(8,128)S(1)} %add.61), channel_id=1, source_target_pairs={{0,4},{1,5},{2,6},{3,7},{4,8},{5,9},{6,10},{7,11},{8,12},{9,13},{1... | collective-permute-start | bytes 1572872 | tf_op jit(solution)/shard_map/ppermute | solution.py:13
  206.5 8.1 %collective-permute-done.8 = f32[8,128,128]{2,1,0:T(8,128)S(1)} collective-permute-done((f32[8,128,128]{2,1,0:T(8,128)S(1)}, f32[8,128,128]{2,1,0:T(8,128)S(1)}, u32[]{:S(2)}, u32[]{:S(2)}) %collective-permute-start.8) | collective-permute-done | bytes 524320 | tf_op jit(solution)/shard_map/ppermute | solution.py:13
  214.7 1.3 collective-permute-start.9
  216.1 1.4 select_convert_fusion.1
  217.5 10.5 %collective-permute-done.2 = f32[8,128,128]{2,1,0:T(8,128)S(1)} collective-permute-done((f32[8,128,128]{2,1,0:T(8,128)S(1)}, f32[8,128,128]{2,1,0:T(8,128)S(1)}, u32[]{:S(2)}, u32[]{:S(2)}) %collective-permute-start.2) | collective-permute-done | bytes 524320 | tf_op jit(solution)/shard_map/ppermute | solution.py:13
  228.0 6.8 %collective-permute-start.3 = (f32[8,128,128]{2,1,0:T(8,128)S(1)}, f32[8,128,128]{2,1,0:T(8,128)S(1)}, u32[]{:S(2)}, u32[]{:S(2)}) collective-permute-start(f32[8,128,128]{2,1,0:T(8,128)S(1)} %add.62), channel_id=1, source_target_pairs={{0,8},{1,9},{2,10},{3,11},{4,12},{5,13},{6,14},{7,15},{8,16},{9,17... | collective-permute-start | bytes 1572872 | tf_op jit(solution)/shard_map/ppermute | solution.py:13
  234.8 12.6 %collective-permute-done.9 = f32[8,128,128]{2,1,0:T(8,128)S(1)} collective-permute-done((f32[8,128,128]{2,1,0:T(8,128)S(1)}, f32[8,128,128]{2,1,0:T(8,128)S(1)}, u32[]{:S(2)}, u32[]{:S(2)}) %collective-permute-start.9) | collective-permute-done | bytes 524320 | tf_op jit(solution)/shard_map/ppermute | solution.py:13
  247.5 1.3 collective-permute-start.10
  248.8 2.0 fusion.14
  250.8 2.8 fusion.27
  254.0 0.8 add.63
  254.8 22.6 %collective-permute-start.4 = (f32[8,128,128]{2,1,0:T(8,128)}, f32[8,128,128]{2,1,0:T(8,128)}, u32[]{:S(2)}, u32[]{:S(2)}) collective-permute-start(f32[8,128,128]{2,1,0:T(8,128)} %add.63), channel_id=1, source_target_pairs={{0,16},{1,17},{2,18},{3,19},{4,20},{5,21},{6,22},{7,23},{8,24},{9,... | collective-permute-start | bytes 1572872 | tf_op jit(solution)/shard_map/ppermute | solution.py:13
  277.4 0.9 add.72
  278.3 1.5 collective-permute-start.11
  279.9 1.0 bitcast_bitcast_fusion
  280.9 4.6 %fusion = f32[8,512,128]{1,2,0:T(8,128)} fusion(pred[512,512]{1,0:T(8,128)(4,1)S(1)} %iota_compare_fusion, bf16[8,512,128]{2,0,1:T(8,128)(2,1)} %bitcast_bitcast_fusion, bf16[1,512,8,128]{1,3,2,0:T(8,128)(2,1)S(1)} %reshape.118, bf16[1,512,8,128]{1,3,2,0:T(8,128)(2,1)S(1)} %reshape.115), kind=kOutput, calls=%fused_computation.2 | convolution fusion | flops 1080033280 | bytes 5505024 | tf_op jit(solution)/shard_map/nhpt,nhpe->nhte/dot_general | solution.py:94
  285.5 2.8 collective-permute-done.4
  288.3 2.0 add.64
  290.3 31.7 %collective-permute-start.5 = (f32[8,128,128]{2,1,0:T(8,128)}, f32[8,128,128]{2,1,0:T(8,128)}, u32[]{:S(2)}, u32[]{:S(2)}) collective-permute-start(f32[8,128,128]{2,1,0:T(8,128)} %add.64), channel_id=1, source_target_pairs={{0,32},{1,33},{2,34},{3,35},{4,36},{5,37},{6,38},{7,39},{8,40},{9,... | collective-permute-start | bytes 1572872 | tf_op jit(solution)/shard_map/ppermute | solution.py:13
  322.1 1.3 collective-permute-done.11
  323.4 1.5 add_convert_fusion
  324.8 1.5 fusion.6
  326.3 2.4 copy.62
  328.7 3.0 fusion.7
  331.7 2.4 copy.61
  334.1 2.9 fusion.8
  337.0 2.3 copy.60
  (32 shorter events, 3.4 us)
Async XLA Ops:
  30.2 36.8 %all-to-all-start = ((bf16[4,2,65536]{2,1,0:T(2,128)(2,1)}), bf16[4,2,65536]{2,1,0:T(2,128)(2,1)S(1)}, u32[]{:S(2)}, u32[]{:S(2)}) async-start(bf16[4,2,65536]{2,1,0:T(2,128)(2,1)} %reshape.124), calls=%async_computation | async-start | bytes 2097152 | tf_op jit(solution)/shard_map/all_to_all | solution.py:39
  67.0 36.7 %all-to-all-start.3 = ((bf16[4,2,65536]{2,1,0:T(2,128)(2,1)}), bf16[4,2,65536]{2,1,0:T(2,128)(2,1)}, u32[]{:S(2)}, u32[]{:S(2)}) async-start(bf16[4,2,65536]{2,1,0:T(2,128)(2,1)} %reshape.128), calls=%async_computation.3 | async-start | bytes 2097152 | tf_op jit(solution)/shard_map/all_to_all | solution.py:36
  103.7 36.7 %all-to-all-start.2 = ((bf16[4,2,65536]{2,1,0:T(2,128)(2,1)}), bf16[4,2,65536]{2,1,0:T(2,128)(2,1)}, u32[]{:S(2)}, u32[]{:S(2)}) async-start(bf16[4,2,65536]{2,1,0:T(2,128)(2,1)} %reshape.126), calls=%async_computation.2 | async-start | bytes 2097152 | tf_op jit(solution)/shard_map/all_to_all | solution.py:37
  140.3 22.9 %all-to-all-start.1 = ((bf16[4,2,65536]{2,1,0:T(2,128)(2,1)}), bf16[4,2,65536]{2,1,0:T(2,128)(2,1)}, u32[]{:S(2)}, u32[]{:S(2)}) async-start(bf16[4,2,65536]{2,1,0:T(2,128)(2,1)} %reshape.122), calls=%async_computation.1 | async-start | bytes 2097152 | tf_op jit(solution)/shard_map/all_to_all | solution.py:38
  152.4 24.2 %collective-permute-start.6 = (f32[8,128,128]{2,1,0:T(8,128)}, f32[8,128,128]{2,1,0:T(8,128)}, u32[]{:S(2)}, u32[]{:S(2)}) collective-permute-start(f32[8,128,128]{2,1,0:T(8,128)} %fusion.12), channel_id=1, source_target_pairs={{1,0},{2,1},{3,2},{4,3},{5,4},{6,5},{7,6},{8,7},{9,8},{10,9},{11,1... | collective-permute-start | bytes 1572872 | tf_op jit(solution)/shard_map/ppermute | solution.py:13
  173.7 42.3 %copy-start = (bf16[64,8,8,128]{3,2,1,0:T(8,128)(2,1)}, bf16[64,8,8,128]{3,2,1,0:T(8,128)(2,1)S(1)}, u32[]{:S(2)}) copy-start(bf16[64,8,8,128]{3,2,1,0:T(8,128)(2,1)S(1)} %copy.75) | copy-start | bytes 3145732
  174.2 19.7 %copy-start.3 = (f32[8,128,128]{2,1,0:T(8,128)}, f32[8,128,128]{2,1,0:T(8,128)S(1)}, u32[]{:S(2)}) copy-start(f32[8,128,128]{2,1,0:T(8,128)S(1)} %fusion.20) | copy-start | bytes 1572868
  174.2 10.5 %collective-permute-start = (f32[8,128,128]{2,1,0:T(8,128)S(1)}, f32[8,128,128]{2,1,0:T(8,128)S(1)}, u32[]{:S(2)}, u32[]{:S(2)}) collective-permute-start(f32[8,128,128]{2,1,0:T(8,128)S(1)} %fusion.20), channel_id=1, source_target_pairs={{0,1},{1,2},{2,3},{3,4},{4,5},{5,6},{6,7},{7,8},{8,9},{9,10},{10,1... | collective-permute-start | bytes 1572872 | tf_op jit(solution)/shard_map/ppermute | solution.py:13
  177.9 16.0 %collective-permute-start.7 = (f32[8,128,128]{2,1,0:T(8,128)S(1)}, f32[8,128,128]{2,1,0:T(8,128)S(1)}, u32[]{:S(2)}, u32[]{:S(2)}) collective-permute-start(f32[8,128,128]{2,1,0:T(8,128)S(1)} %add.68), channel_id=1, source_target_pairs={{2,0},{3,1},{4,2},{5,3},{6,4},{7,5},{8,6},{9,7},{10,8},{11,9},{12,... | collective-permute-start | bytes 1572872 | tf_op jit(solution)/shard_map/ppermute | solution.py:13
  184.8 15.3 %collective-permute-start.1 = (f32[8,128,128]{2,1,0:T(8,128)S(1)}, f32[8,128,128]{2,1,0:T(8,128)S(1)}, u32[]{:S(2)}, u32[]{:S(2)}) collective-permute-start(f32[8,128,128]{2,1,0:T(8,128)S(1)} %add.60), channel_id=1, source_target_pairs={{0,2},{1,3},{2,4},{3,5},{4,6},{5,7},{6,8},{7,9},{8,10},{9,11},{10,... | collective-permute-start | bytes 1572872 | tf_op jit(solution)/shard_map/ppermute | solution.py:13
  193.9 20.7 %collective-permute-start.8 = (f32[8,128,128]{2,1,0:T(8,128)S(1)}, f32[8,128,128]{2,1,0:T(8,128)S(1)}, u32[]{:S(2)}, u32[]{:S(2)}) collective-permute-start(f32[8,128,128]{2,1,0:T(8,128)S(1)} %add.69), channel_id=1, source_target_pairs={{4,0},{5,1},{6,2},{7,3},{8,4},{9,5},{10,6},{11,7},{12,8},{13,9},{1... | collective-permute-start | bytes 1572872 | tf_op jit(solution)/shard_map/ppermute | solution.py:13
  200.1 27.9 %collective-permute-start.2 = (f32[8,128,128]{2,1,0:T(8,128)S(1)}, f32[8,128,128]{2,1,0:T(8,128)S(1)}, u32[]{:S(2)}, u32[]{:S(2)}) collective-permute-start(f32[8,128,128]{2,1,0:T(8,128)S(1)} %add.61), channel_id=1, source_target_pairs={{0,4},{1,5},{2,6},{3,7},{4,8},{5,9},{6,10},{7,11},{8,12},{9,13},{1... | collective-permute-start | bytes 1572872 | tf_op jit(solution)/shard_map/ppermute | solution.py:13
  214.7 32.7 %collective-permute-start.9 = (f32[8,128,128]{2,1,0:T(8,128)S(1)}, f32[8,128,128]{2,1,0:T(8,128)S(1)}, u32[]{:S(2)}, u32[]{:S(2)}) collective-permute-start(f32[8,128,128]{2,1,0:T(8,128)S(1)} %add.70), channel_id=1, source_target_pairs={{8,0},{9,1},{10,2},{11,3},{12,4},{13,5},{14,6},{15,7},{16,8},{17,9... | collective-permute-start | bytes 1572872 | tf_op jit(solution)/shard_map/ppermute | solution.py:13
  228.0 26.0 %collective-permute-start.3 = (f32[8,128,128]{2,1,0:T(8,128)S(1)}, f32[8,128,128]{2,1,0:T(8,128)S(1)}, u32[]{:S(2)}, u32[]{:S(2)}) collective-permute-start(f32[8,128,128]{2,1,0:T(8,128)S(1)} %add.62), channel_id=1, source_target_pairs={{0,8},{1,9},{2,10},{3,11},{4,12},{5,13},{6,14},{7,15},{8,16},{9,17... | collective-permute-start | bytes 1572872 | tf_op jit(solution)/shard_map/ppermute | solution.py:13
  247.5 30.0 %collective-permute-start.10 = (f32[8,128,128]{2,1,0:T(8,128)S(1)}, f32[8,128,128]{2,1,0:T(8,128)S(1)}, u32[]{:S(2)}, u32[]{:S(2)}) collective-permute-start(f32[8,128,128]{2,1,0:T(8,128)S(1)} %add.71), channel_id=1, source_target_pairs={{16,0},{17,1},{18,2},{19,3},{20,4},{21,5},{22,6},{23,7},{24,8},{25... | collective-permute-start | bytes 1572872 | tf_op jit(solution)/shard_map/ppermute | solution.py:13
  254.8 33.4 %collective-permute-start.4 = (f32[8,128,128]{2,1,0:T(8,128)}, f32[8,128,128]{2,1,0:T(8,128)}, u32[]{:S(2)}, u32[]{:S(2)}) collective-permute-start(f32[8,128,128]{2,1,0:T(8,128)} %add.63), channel_id=1, source_target_pairs={{0,16},{1,17},{2,18},{3,19},{4,20},{5,21},{6,22},{7,23},{8,24},{9,... | collective-permute-start | bytes 1572872 | tf_op jit(solution)/shard_map/ppermute | solution.py:13
  278.3 45.0 %collective-permute-start.11 = (f32[8,128,128]{2,1,0:T(8,128)}, f32[8,128,128]{2,1,0:T(8,128)}, u32[]{:S(2)}, u32[]{:S(2)}) collective-permute-start(f32[8,128,128]{2,1,0:T(8,128)} %add.72), channel_id=1, source_target_pairs={{32,0},{33,1},{34,2},{35,3},{36,4},{37,5},{38,6},{39,7},{40,8},{41... | collective-permute-start | bytes 1572872 | tf_op jit(solution)/shard_map/ppermute | solution.py:13
  285.5 39.3 %copy-start.4 = (f32[8,512,128]{1,2,0:T(8,128)S(1)}, f32[8,512,128]{1,2,0:T(8,128)}, u32[]{:S(2)}) copy-start(f32[8,512,128]{1,2,0:T(8,128)} %fusion) | copy-start | bytes 6291460
  290.3 43.8 %collective-permute-start.5 = (f32[8,128,128]{2,1,0:T(8,128)}, f32[8,128,128]{2,1,0:T(8,128)}, u32[]{:S(2)}, u32[]{:S(2)}) collective-permute-start(f32[8,128,128]{2,1,0:T(8,128)} %add.64), channel_id=1, source_target_pairs={{0,32},{1,33},{2,34},{3,35},{4,36},{5,37},{6,38},{7,39},{8,40},{9,... | collective-permute-start | bytes 1572872 | tf_op jit(solution)/shard_map/ppermute | solution.py:13
  326.3 2.4 copy-start.1
  331.7 2.4 copy-start.2
where the time goes:
time: 341 us; the launch traced here: 339 us
  starting transfers between devices  103 us (30%)
  other arithmetic  99.4 us (29%)
  local copies, waits for them, and re-layouts  66.1 us (19%)
  waiting for transfers between devices  49.7 us (15%)
  matrix products  19.9 us (6%)
    unnamed x4, other arithmetic  92.4 us
    ppermute x12, starting transfers between devices, shifted(): lax.ppermute(value, axis, [(source, source + steps) for source in range(l...  83.9 us
    unnamed x32, local copies, waits for them, and re-layouts  57.8 us
    ppermute x12, waiting for transfers between devices, shifted(): lax.ppermute(value, axis, [(source, source + steps) for source in range(l...  49.7 us
  transfers between devices with their start and end apart: 16, of which 9 were waited for; matrix products, arithmetic and copies ran while one was open for 44% of the time, Pallas kernels for 0%

commit v1 on v0

v1 whole, which is shorter than its diff:
```python
import functools

import jax
import jax.numpy as jnp
from jax import lax
from jax.experimental import pallas as pl
from jax.experimental.pallas import tpu as pltpu
from jax.sharding import PartitionSpec as P

HD = 128
BLOCK = 512
HALF = 256
MESH = pl.DeviceIdType.MESH
NT = (((1,), (1,)), ((), ()))
NN = (((1,), (0,)), ((), ()))
TN = (((0,), (0,)), ((), ()))
WINDOW = 8


def dot(a, b, dims):
    return lax.dot_general(a, b, dims, preferred_element_type=jnp.float32)


def kernel(
    heads, nx, row, factor,
    q_in, k_in, v_in, g_in, gq_out, gk_out, gv_out,
    xin, acc, own, gat, tot, pre, st,
    y_send, y_recv, y_loc, a_send, a_recv, b_send, b_recv, c_send, c_recv,
):
    ny = lax.axis_size("head")
    y = lax.axis_index("head")
    ctx = lax.axis_index("ctx")
    x = ctx // row
    me = ctx % row
    is_q = me // (row // 2)
    rows_y = BLOCK // ny
    ins = (q_in, k_in, v_in, g_in)
    per = 2 * HD // row
    dists = (2, 1, 3)

    def row_peer(d):
        t = lax.rem(me + d, row)
        return t, {"ctx": x * row + t}

    def x_peer(d):
        return {"ctx": lax.rem(x + d, nx) * row + me}

    barrier = pltpu.get_barrier_semaphore()
    for d in dists:
        pl.semaphore_signal(barrier, inc=1, device_id={"head": lax.rem(y + d, ny)}, device_id_type=MESH)
    for d in range(1, row):
        pl.semaphore_signal(barrier, inc=1, device_id=row_peer(d)[1], device_id_type=MESH)
    for d in range(1, nx):
        pl.semaphore_signal(barrier, inc=1, device_id=x_peer(d), device_id_type=MESH)
    pl.semaphore_wait(barrier, ny - 1 + row - 1 + nx - 1)

    def my_rows(owner):
        return pl.ds(pl.multiple_of(owner * rows_y, rows_y), rows_y)

    def cols(owner, h):
        return pl.ds(pl.multiple_of((owner * heads + h) * HD, HD), HD)

    def send_y(h):
        for d in dists:
            tgt = lax.rem(y + d, ny)
            for a in range(4):
                pltpu.make_async_remote_copy(
                    src_ref=ins[a].at[0, :, cols(tgt, h)],
                    dst_ref=xin.at[h, a, my_rows(y), :],
                    send_sem=y_send.at[h],
                    recv_sem=y_recv.at[h],
                    device_id={"head": tgt},
                    device_id_type=MESH,
                ).start()
        for a in range(4):
            pltpu.make_async_copy(
                ins[a].at[0, :, cols(y, h)], xin.at[h, a, my_rows(y), :], y_loc.at[h]
            ).start()

    def wait_bytes(ref, sem):
        pltpu.make_async_copy(ref, ref, sem).wait()

    def states(h):
        wait_bytes(xin.at[h, 0 : ny - 1], y_recv.at[h])
        wait_bytes(xin.at[h, 0:1], y_loc.at[h])
        own[h, 0:HD, :] = dot(xin[h, 1], xin[h, 2], TN)
        own[h, HD : 2 * HD, :] = dot(xin[h, 0], xin[h, 3], TN)
        for d in range(1, row):
            t, peer = row_peer(d)
            pltpu.make_async_remote_copy(
                src_ref=own.at[h, pl.ds(pl.multiple_of(t * per, per), per), :],
                dst_ref=gat.at[h, me],
                send_sem=a_send.at[h],
                recv_sem=a_recv.at[h],
                device_id=peer,
                device_id_type=MESH,
            ).start()
        gat[h, me] = own[h, pl.ds(pl.multiple_of(me * per, per), per), :]

    def totals(h):
        wait_bytes(gat.at[h, 0 : row - 1], a_recv.at[h])
        total = gat[h, 0]
        for s in range(1, row):
            total = total + gat[h, s]
        tot[h, x] = total
        for d in range(1, nx):
            pltpu.make_async_remote_copy(
                src_ref=tot.at[h, x],
                dst_ref=tot.at[h, x],
                send_sem=b_send.at[h],
                recv_sem=b_recv.at[h],
                device_id=x_peer(d),
                device_id_type=MESH,
            ).start()

    def prefixes(h):
        wait_bytes(tot.at[h, 0 : nx - 1], b_recv.at[h])
        run = jnp.zeros((per, HD), jnp.float32)
        for s in range(nx):
            before = (s - x) * (2 * is_q - 1) > 0
            run = run + jnp.where(before, tot[h, s], 0.0)
        for s in range(row):
            at = s + is_q * (row - 1 - 2 * s)
            pre[h, at] = run.astype(jnp.bfloat16)
            run = run + gat[h, at]
        for d in range(1, row):
            t, peer = row_peer(d)
            pltpu.make_async_remote_copy(
                src_ref=pre.at[h, t],
                dst_ref=st.at[h, me],
                send_sem=c_send.at[h],
                recv_sem=c_recv.at[h],
                device_id=peer,
                device_id_type=MESH,
            ).start()
        st[h, me] = pre[h, me]

    r_at = lax.broadcasted_iota(jnp.int32, (HALF, HALF), 0)
    c_at = lax.broadcasted_iota(jnp.int32, (HALF, HALF), 1)

    def causal(h):
        lo, hi = pl.ds(0, HALF), pl.ds(HALF, HALF)

        def low(s):
            return jnp.where(r_at >= c_at, s, 0.0).astype(jnp.bfloat16)

        def upp(s):
            return jnp.where(r_at <= c_at, s, 0.0).astype(jnp.bfloat16)

        def part(a, at):
            return xin[h, a, at, :]

        def scores(left, right, first, other, last):
            s_first = dot(part(left, lo), part(right, lo), NT)
            s_last = dot(part(left, hi), part(right, hi), NT)
            s_other = dot(part(left, first), part(right, last), NT)
            return other(s_first), s_other.astype(jnp.bfloat16), other(s_last)

        a00, a10, a11 = scores(3, 2, hi, low, lo)
        acc[h, 0, lo, :] = dot(a00, part(1, lo), NN)
        acc[h, 0, hi, :] = dot(a10, part(1, lo), NN) + dot(a11, part(1, hi), NN)
        t00, t01, t11 = scores(2, 3, lo, upp, hi)
        acc[h, 1, lo, :] = dot(t00, part(0, lo), NN) + dot(t01, part(0, hi), NN)
        acc[h, 1, hi, :] = dot(t11, part(0, hi), NN)
        b00, b01, b11 = scores(1, 0, lo, upp, hi)
        acc[h, 2, lo, :] = dot(b00, part(3, lo), NN) + dot(b01, part(3, hi), NN)
        acc[h, 2, hi, :] = dot(b11, part(3, hi), NN)

    def finish(h):
        wait_bytes(st.at[h, 0 : row - 1], c_recv.at[h])
        ks = st[h, 0 : row // 2].reshape(HD, HD)
        qs = st[h, row // 2 : row].reshape(HD, HD)
        at = pl.ds(pl.multiple_of(h * HD, HD), HD)
        gq_out[0, :, at] = (factor * (acc[h, 0] + dot(xin[h, 3], ks, NT))).astype(jnp.bfloat16)
        gk_out[0, :, at] = (factor * (acc[h, 1] + dot(xin[h, 2], qs, NT))).astype(jnp.bfloat16)
        gv_out[0, :, at] = (factor * (acc[h, 2] + dot(xin[h, 1], qs, NN))).astype(jnp.bfloat16)

    @pl.loop(0, min(WINDOW, heads))
    def _(h):
        send_y(h)

    @pl.loop(0, heads)
    def _(h):
        if WINDOW < heads:
            @pl.when(h + WINDOW < heads)
            def _():
                send_y(h + WINDOW)

        states(h)
        causal(h)

        @pl.when(h >= 1)
        def _():
            totals(h - 1)

        @pl.when(h >= 2)
        def _():
            prefixes(h - 2)

        @pl.when(h >= 3)
        def _():
            finish(h - 3)

    prefixes(heads - 2)
    finish(heads - 3)
    totals(heads - 1)
    finish(heads - 2)
    prefixes(heads - 1)
    finish(heads - 1)

    @pl.loop(0, heads)
    def _(h):
        wait_bytes(xin.at[h, 0 : ny - 1], y_send.at[h])
        wait_bytes(gat.at[h, 0 : row - 1], a_send.at[h])
        wait_bytes(tot.at[h, 0 : nx - 1], b_send.at[h])
        wait_bytes(st.at[h, 0 : row - 1], c_send.at[h])


def shards(nx, query, keys, values, grad_out):
    ny = lax.axis_size("head")
    nctx = lax.axis_size("ctx")
    row = nctx // nx
    heads = query.shape[2] // ny // HD
    factor = (HD * BLOCK * nctx) ** (-0.5)
    per = 2 * HD // row
    dma = pltpu.SemaphoreType.DMA((heads,))
    flops = heads * (9 * 2 * BLOCK * BLOCK * HD * 3 // 4 + 5 * 2 * BLOCK * HD * HD)
    ins = [pltpu.with_memory_space_constraint(a, pltpu.HBM) for a in (query, keys, values, grad_out)]
    return pl.pallas_call(
        functools.partial(kernel, heads, nx, row, factor),
        out_shape=[pltpu.VMEM((1, BLOCK, heads * HD), jnp.bfloat16)] * 3,
        in_specs=[pl.BlockSpec(memory_space=pltpu.HBM)] * 4,
        out_specs=[pl.BlockSpec(memory_space=pltpu.VMEM)] * 3,
        scratch_shapes=[
            pltpu.VMEM((heads, 4, BLOCK, HD), jnp.bfloat16),
            pltpu.VMEM((heads, 3, BLOCK, HD), jnp.float32),
            pltpu.VMEM((heads, 2 * HD, HD), jnp.float32),
            pltpu.VMEM((heads, row, per, HD), jnp.float32),
            pltpu.VMEM((heads, nx, per, HD), jnp.float32),
            pltpu.VMEM((heads, row, per, HD), jnp.bfloat16),
            pltpu.VMEM((heads, row, per, HD), jnp.bfloat16),
        ]
        + [dma] * 9,
        compiler_params=pltpu.CompilerParams(
            collective_id=1, has_side_effects=True, vmem_limit_bytes=40 * 2**20
        ),
        cost_estimate=pl.CostEstimate(flops=flops, bytes_accessed=8 * 2**20, transcendentals=0),
    )(*ins)


def solution(mesh):
    nx = 4
    in_specs = (P("ctx", "head", None),) * 4
    out_specs = (P("ctx", None, "head"),) * 3
    return jax.shard_map(
        functools.partial(shards, nx), mesh=mesh, in_specs=in_specs, out_specs=out_specs, check_vma=False
    )
```

time: 341 us -> 81 us (0.24)
  the two profiles are of different devices: /device:TPU:40 before, /device:TPU:1 now
where the time goes in v1:
time: 81 us; the launch traced here: 80.9 us
  Pallas kernels  77.3 us (95%)
  local copies, waits for them, and re-layouts  2.91 us (4%)
    pallas_call x1, Pallas kernels, shards(): pl.pallas_call(functools.partial(kernel, heads, nx, row, factor), out_sha...  77.3 us
    unnamed x3, local copies, waits for them, and re-layouts  2.91 us

profile of v1, /device:TPU:1, one launch (start us, length us, event | category | flops | bytes accessed | tf_op | source)
XLA Modules:
  0.0 80.9 jit_solution(3931705460339039141)
XLA Ops:
  0.6 77.3 %shard_map.67 = (bf16[1,512,1024]{2,1,0:T(8,128)(2,1)S(1)}, bf16[1,512,1024]{2,1,0:T(8,128)(2,1)S(1)}, bf16[1,512,1024]{2,1,0:T(8,128)(2,1)S(1)}) custom-call(bf16[1,128,4096]{2,1,0:T(8,128)(2,1)} %q_in.1, bf16[1,128,4096]{2,1,0:T(8,128)(2,1)} %k_in.1, bf16[1,128,4096]{2,1,0:T(8,128)(2,1)} %v_in.1, bf16[1,128,4096]{2,1,0:T(8,128)(2,1)} %g_in.1), custom_call_target="tpu_custom_call" | custom-call | flops 4294967296 | bytes 8388608 | tf_op jit(solution)/shard_map/pallas_call | solution.py:229
  78.0 1.0 %copy.10 = bf16[1,512,1024]{2,1,0:T(8,128)(2,1)} copy(bf16[1,512,1024]{2,1,0:T(8,128)(2,1)S(1)} %get-tuple-element.3) | data formatting | bytes 2097152
  79.0 1.0 %copy.11 = bf16[1,512,1024]{2,1,0:T(8,128)(2,1)} copy(bf16[1,512,1024]{2,1,0:T(8,128)(2,1)S(1)} %get-tuple-element.4) | data formatting | bytes 2097152
  79.9 1.0 %copy.12 = bf16[1,512,1024]{2,1,0:T(8,128)(2,1)} copy(bf16[1,512,1024]{2,1,0:T(8,128)(2,1)S(1)} %get-tuple-element.5) | data formatting | bytes 2097152

commit v2 on v1

v2 whole, which is shorter than its diff:
```python
import functools

import jax
import jax.numpy as jnp
from jax import lax
from jax.experimental import pallas as pl
from jax.experimental.pallas import tpu as pltpu
from jax.sharding import PartitionSpec as P

HD = 128
BLOCK = 512
HALF = 256
MESH = pl.DeviceIdType.MESH
NT = (((1,), (1,)), ((), ()))
NN = (((1,), (0,)), ((), ()))
TN = (((0,), (0,)), ((), ()))
WINDOW = 4
BEFORE = 1
EARLY = 3
AT_SUM, AT_TOTAL, AT_PREFIX = 0, 1, 2
LAG_TOTAL, LAG_PREFIX, LAG_FINISH = 1, 2, 3


def dot(a, b, dims):
    return lax.dot_general(a, b, dims, preferred_element_type=jnp.float32)


def kernel(
    heads, nx, row, factor,
    q_in, k_in, v_in, g_in, gq_out, gk_out, gv_out,
    xin, acc, own, gat, tot, pre, st,
    ear, psend, precv, chip, egat, etot, epre, est, mate,
    rounds, y_send, y_recv, y_loc, a_send, a_recv, b_send, b_recv, c_send, c_recv,
    m_send, m_recv, e_loc, e_send, e_recv, p_send, p_recv,
    ea_send, ea_recv, eb_send, eb_recv, ec_send, ec_recv,
):
    ny = lax.axis_size("head")
    y = lax.axis_index("head")
    ctx = lax.axis_index("ctx")
    nz = row // 2
    x = ctx // row
    me = ctx % row
    z = me // 2
    core = me % 2
    is_q = me // nz
    rows_y = BLOCK // ny
    ins = (q_in, k_in, v_in, g_in)
    per = 2 * HD // row
    early = ear.shape[3] // HD
    normal = heads - early
    dists = (2, 1, 3)

    def y_peer(d):
        return {"head": lax.rem(y + d, ny)}

    def place(x_at, z_at, core_at):
        return {"ctx": (x_at * nz + z_at) * 2 + core_at}

    def row_peer(d):
        t = lax.rem(me + d, row)
        return t, {"ctx": x * row + t}

    def x_peer(d):
        return {"ctx": lax.rem(x + d, nx) * row + me}

    partner = place(x, z, 1 - core)
    z_next = [place(x, lax.rem(z + d, nz), core) for d in (1, nz - 1)]
    x_next = [x_peer(d) for d in (1, nx - 1)]
    near = [y_peer(d) for d in dists] + [partner] + z_next + x_next

    def signal(sem, device):
        pl.semaphore_signal(sem, inc=1, device_id=device, device_id_type=MESH)

    barrier = pltpu.get_barrier_semaphore()
    for device in near:
        signal(barrier, device)
    pl.semaphore_wait(barrier, len(near))

    def remote(src, dst, send, recv, device):
        pltpu.make_async_remote_copy(
            src_ref=src, dst_ref=dst, send_sem=send, recv_sem=recv,
            device_id=device, device_id_type=MESH,
        ).start()

    def wait_bytes(ref, sem):
        pltpu.make_async_copy(ref, ref, sem).wait()

    def my_rows(owner):
        return pl.ds(pl.multiple_of(owner * rows_y, rows_y), rows_y)

    def cols(owner, h, count=1):
        return pl.ds(pl.multiple_of((owner * heads + h) * HD, HD), count * HD)

    def send_y(h):
        for d in dists:
            tgt = lax.rem(y + d, ny)
            for a in range(4):
                remote(
                    ins[a].at[0, :, cols(tgt, h)], xin.at[h, a, my_rows(y), :],
                    y_send.at[h], y_recv.at[h], {"head": tgt},
                )
        for a in range(4):
            pltpu.make_async_copy(
                ins[a].at[0, :, cols(y, h)], xin.at[h, a, my_rows(y), :], y_loc.at[h]
            ).start()

    def early_rows():
        at = pl.ds(pl.multiple_of(core * rows_y, rows_y), rows_y)
        keys_side, query_side = (k_in, v_in), (q_in, g_in)

        def go(keep, give):
            for t in range(ny):
                for i in range(2):
                    src = (0, slice(None), cols(t, normal, early))
                    dst = ear.at[i, t, at, :]
                    remote(give[i].at[src], dst, e_send, e_recv, partner)
                    pltpu.make_async_copy(keep[i].at[src], dst, e_loc).start()

        @pl.when(core == 0)
        def _():
            go(keys_side, query_side)

        @pl.when(core == 1)
        def _():
            go(query_side, keys_side)

    def early_parts():
        wait_bytes(ear.at[0], e_loc)
        wait_bytes(ear.at[0], e_recv)
        for d in (2, 1, 3, 0):
            t = lax.rem(y + d, ny)
            for e in range(early):
                at = slice(e * HD, (e + 1) * HD)
                part = dot(ear[0, t, :, at], ear[1, t, :, at], TN)
                if d:
                    psend[d, e] = part.astype(jnp.bfloat16)
                else:
                    chip[:, e] = part.reshape(nz, per, HD)
            if d:
                remote(psend.at[d], precv.at[y], p_send, p_recv, y_peer(d))

    def early_sum():
        wait_bytes(precv.at[0 : ny - 1], p_recv)
        for e in range(early):
            total = chip[:, e]
            for d in range(1, ny):
                got = precv[lax.rem(y + d, ny), e].astype(jnp.float32)
                total = total + got.reshape(nz, per, HD)
            chip[:, e] = total
        for d in range(1, nz):
            t = lax.rem(z + d, nz)
            remote(chip.at[t], egat.at[z], ea_send, ea_recv, place(x, t, core))
        egat[z] = chip[z]

    def early_totals():
        wait_bytes(egat.at[0 : nz - 1], ea_recv)
        total = egat[0]
        for s in range(1, nz):
            total = total + egat[s]
        etot[x] = total
        for d in range(1, nx):
            remote(etot.at[x], etot.at[x], eb_send, eb_recv, x_peer(d))

    def base(parts, x_side):
        run = jnp.zeros(parts.shape[1:], jnp.float32)
        for s in range(nx):
            run = run + jnp.where((s - x) * x_side > 0, parts[s], 0.0)
        return run

    def early_prefixes():
        wait_bytes(etot.at[0 : nx - 1], eb_recv)
        run = base(etot, 2 * core - 1)
        for s in range(nz):
            at = s + core * (nz - 1 - 2 * s)
            epre[at] = run
            run = run + egat[at]
        mine = core * nz + z
        for d in range(1, row):
            t, peer = row_peer(d)
            remote(epre.at[t // 2], est.at[mine], ec_send, ec_recv, peer)
        est[mine] = epre[z]

    def wait_y(h):
        wait_bytes(xin.at[h, 0 : ny - 1], y_recv.at[h])
        wait_bytes(xin.at[h, 0:1], y_loc.at[h])

    def states(h):
        own[h, 0:HD, :] = dot(xin[h, 1], xin[h, 2], TN)
        own[h, HD : 2 * HD, :] = dot(xin[h, 0], xin[h, 3], TN)
        for d in range(1, row):
            t, peer = row_peer(d)
            src = own.at[h, pl.ds(pl.multiple_of(t * per, per), per), :]
            remote(src, gat.at[h, me], a_send.at[h], a_recv.at[h], peer)
        gat[h, me] = own[h, pl.ds(pl.multiple_of(me * per, per), per), :]

    def late_state(h):
        e = h - normal
        mate[0, e] = dot(xin[h, 1 - core], xin[h, 2 + core], TN)
        remote(mate.at[0, e], mate.at[1, e], m_send.at[e], m_recv.at[e], partner)

    def totals(h):
        wait_bytes(gat.at[h, 0 : row - 1], a_recv.at[h])
        total = gat[h, 0]
        for s in range(1, row):
            total = total + gat[h, s]
        tot[h, x] = total
        for d in range(1, nx):
            remote(tot.at[h, x], tot.at[h, x], b_send.at[h], b_recv.at[h], x_peer(d))

    def prefixes(h):
        wait_bytes(tot.at[h, 0 : nx - 1], b_recv.at[h])
        run = base(tot.at[h], 2 * is_q - 1)
        for s in range(row):
            at = s + is_q * (row - 1 - 2 * s)
            pre[h, at] = run.astype(jnp.bfloat16)
            run = run + gat[h, at]
        for d in range(1, row):
            t, peer = row_peer(d)
            remote(pre.at[h, t], st.at[h, me], c_send.at[h], c_recv.at[h], peer)
        st[h, me] = pre[h, me]

    r_at = lax.broadcasted_iota(jnp.int32, (HALF, HALF), 0)
    c_at = lax.broadcasted_iota(jnp.int32, (HALF, HALF), 1)

    def causal(h):
        lo, hi = pl.ds(0, HALF), pl.ds(HALF, HALF)

        def low(s):
            return jnp.where(r_at >= c_at, s, 0.0).astype(jnp.bfloat16)

        def upp(s):
            return jnp.where(r_at <= c_at, s, 0.0).astype(jnp.bfloat16)

        def part(a, at):
            return xin[h, a, at, :]

        def scores(left, right, first, other, last):
            s_first = dot(part(left, lo), part(right, lo), NT)
            s_last = dot(part(left, hi), part(right, hi), NT)
            s_other = dot(part(left, first), part(right, last), NT)
            return other(s_first), s_other.astype(jnp.bfloat16), other(s_last)

        a00, a10, a11 = scores(3, 2, hi, low, lo)
        acc[h, 0, lo, :] = dot(a00, part(1, lo), NN)
        acc[h, 0, hi, :] = dot(a10, part(1, lo), NN) + dot(a11, part(1, hi), NN)
        t00, t01, t11 = scores(2, 3, lo, upp, hi)
        acc[h, 1, lo, :] = dot(t00, part(0, lo), NN) + dot(t01, part(0, hi), NN)
        acc[h, 1, hi, :] = dot(t11, part(0, hi), NN)
        b00, b01, b11 = scores(1, 0, lo, upp, hi)
        acc[h, 2, lo, :] = dot(b00, part(3, lo), NN) + dot(b01, part(3, hi), NN)
        acc[h, 2, hi, :] = dot(b11, part(3, hi), NN)

    def finish(h, ks, qs):
        at = pl.ds(pl.multiple_of(h * HD, HD), HD)
        gq_out[0, :, at] = (factor * (acc[h, 0] + dot(xin[h, 3], ks, NT))).astype(jnp.bfloat16)
        gk_out[0, :, at] = (factor * (acc[h, 1] + dot(xin[h, 2], qs, NT))).astype(jnp.bfloat16)
        gv_out[0, :, at] = (factor * (acc[h, 2] + dot(xin[h, 1], qs, NN))).astype(jnp.bfloat16)

    def finish_normal(h):
        wait_bytes(st.at[h, 0 : row - 1], c_recv.at[h])
        ks = st[h, 0 : row // 2].reshape(HD, HD)
        qs = st[h, row // 2 : row].reshape(HD, HD)
        finish(h, ks, qs)

    def finish_early(h):
        e = h - normal
        wait_bytes(mate.at[0, e], m_recv.at[e])
        late = mate[1, e]
        ks = est[0:nz, e].reshape(HD, HD) + jnp.where(core == 1, late, 0.0)
        qs = est[nz : 2 * nz, e].reshape(HD, HD) + jnp.where(core == 0, late, 0.0)
        finish(h, ks.astype(jnp.bfloat16), qs.astype(jnp.bfloat16))

    for h in range(min(WINDOW, BEFORE)):
        send_y(h)
    early_rows()
    for r in range(rounds.shape[0]):
        for device in z_next + x_next:
            signal(rounds.at[r], device)
        if r == 0:
            early_parts()
            for h in range(BEFORE, min(WINDOW, heads)):
                send_y(h)
        pl.semaphore_wait(rounds.at[r], 4)

    @pl.loop(0, heads)
    def _(h):
        @pl.when(h + WINDOW < heads)
        def _():
            send_y(h + WINDOW)

        wait_y(h)

        @pl.when(h < normal)
        def _():
            states(h)

        @pl.when(h >= normal)
        def _():
            late_state(h)

        @pl.when(h == AT_SUM)
        def _():
            early_sum()

        causal(h)

        def lagged(lag, first, end, fn):
            @pl.when((h - lag >= first) & (h - lag < end))
            def _():
                fn(h - lag)

        lagged(LAG_TOTAL, 0, normal, totals)

        @pl.when(h == AT_TOTAL)
        def _():
            early_totals()

        lagged(LAG_PREFIX, 0, normal, prefixes)

        @pl.when(h == AT_PREFIX)
        def _():
            early_prefixes()

        lagged(LAG_FINISH, 0, normal, finish_normal)

        @pl.when(h == normal)
        def _():
            wait_bytes(est.at[0 : row - 1], ec_recv)

        lagged(1, normal, heads, finish_early)

    finish_early(heads - 1)

    wait_bytes(ear.at[0], e_send)
    wait_bytes(precv.at[0 : ny - 1], p_send)
    wait_bytes(egat.at[0 : nz - 1], ea_send)
    wait_bytes(etot.at[0 : nx - 1], eb_send)
    wait_bytes(est.at[0 : row - 1], ec_send)

    @pl.loop(0, heads)
    def _(h):
        wait_bytes(xin.at[h, 0 : ny - 1], y_send.at[h])

    @pl.loop(0, normal)
    def _(h):
        wait_bytes(gat.at[h, 0 : row - 1], a_send.at[h])
        wait_bytes(tot.at[h, 0 : nx - 1], b_send.at[h])
        wait_bytes(st.at[h, 0 : row - 1], c_send.at[h])

    @pl.loop(0, early)
    def _(e):
        wait_bytes(mate.at[0, e], m_send.at[e])


def shards(nx, query, keys, values, grad_out):
    ny = lax.axis_size("head")
    nctx = lax.axis_size("ctx")
    row = nctx // nx
    nz = row // 2
    heads = query.shape[2] // ny // HD
    factor = (HD * BLOCK * nctx) ** (-0.5)
    per = 2 * HD // row
    early = min(EARLY, heads - 1)
    normal = heads - early
    dma = pltpu.SemaphoreType.DMA
    flops = heads * (9 * 2 * BLOCK * BLOCK * HD * 3 // 4 + 5 * 2 * BLOCK * HD * HD)
    ins = [pltpu.with_memory_space_constraint(a, pltpu.HBM) for a in (query, keys, values, grad_out)]
    f32, bf16 = jnp.float32, jnp.bfloat16
    return pl.pallas_call(
        functools.partial(kernel, heads, nx, row, factor),
        out_shape=[pltpu.VMEM((1, BLOCK, heads * HD), bf16)] * 3,
        in_specs=[pl.BlockSpec(memory_space=pltpu.HBM)] * 4,
        out_specs=[pl.BlockSpec(memory_space=pltpu.VMEM)] * 3,
        scratch_shapes=[
            pltpu.VMEM((heads, 4, BLOCK, HD), bf16),
            pltpu.VMEM((heads, 3, BLOCK, HD), f32),
            pltpu.VMEM((normal, 2 * HD, HD), f32),
            pltpu.VMEM((normal, row, per, HD), f32),
            pltpu.VMEM((normal, nx, per, HD), f32),
            pltpu.VMEM((normal, row, per, HD), bf16),
            pltpu.VMEM((normal, row, per, HD), bf16),
            pltpu.VMEM((2, ny, 2 * BLOCK // ny, early * HD), bf16),
            pltpu.VMEM((ny, early, HD, HD), bf16),
            pltpu.VMEM((ny, early, HD, HD), bf16),
            pltpu.VMEM((nz, early, per, HD), f32),
            pltpu.VMEM((nz, early, per, HD), f32),
            pltpu.VMEM((nx, early, per, HD), f32),
            pltpu.VMEM((nz, early, per, HD), f32),
            pltpu.VMEM((row, early, per, HD), f32),
            pltpu.VMEM((2, early, HD, HD), f32),
            pltpu.SemaphoreType.REGULAR((nz // 2,)),
        ]
        + [dma((heads,))] * 3
        + [dma((normal,))] * 6
        + [dma((early,))] * 2
        + [dma] * 11,
        compiler_params=pltpu.CompilerParams(
            collective_id=1, has_side_effects=True, vmem_limit_bytes=44 * 2**20
        ),
        cost_estimate=pl.CostEstimate(flops=flops, bytes_accessed=8 * 2**20, transcendentals=0),
    )(*ins)


def solution(mesh):
    nx = 4
    in_specs = (P("ctx", "head", None),) * 4
    out_specs = (P("ctx", None, "head"),) * 3
    return jax.shard_map(
        functools.partial(shards, nx), mesh=mesh, in_specs=in_specs, out_specs=out_specs, check_vma=False
    )
```

time: 81 us -> 71.5 us (0.88)
  Pallas kernels: 77.3 us -> 67.8 us
    pallas_call x1, Pallas kernels: 77.3 us -> 67.8 us  [shards(): pl.pallas_call(functools.partial(kernel, heads, nx, row, factor), out_sha...]
where the time goes in v2:
time: 71.5 us; the launch traced here: 71.4 us
  Pallas kernels  67.8 us (95%)
  local copies, waits for them, and re-layouts  2.91 us (4%)
    pallas_call x1, Pallas kernels, shards(): pl.pallas_call(functools.partial(kernel, heads, nx, row, factor), out_sha...  67.8 us
    unnamed x3, local copies, waits for them, and re-layouts  2.91 us

profile of v2, /device:TPU:1, one launch (start us, length us, event | category | flops | bytes accessed | tf_op | source)
XLA Modules:
  0.0 71.4 jit_solution(407606299941494953)
XLA Ops:
  0.6 67.8 %shard_map.67 = (bf16[1,512,1024]{2,1,0:T(8,128)(2,1)S(1)}, bf16[1,512,1024]{2,1,0:T(8,128)(2,1)S(1)}, bf16[1,512,1024]{2,1,0:T(8,128)(2,1)S(1)}) custom-call(bf16[1,128,4096]{2,1,0:T(8,128)(2,1)} %q_in.1, bf16[1,128,4096]{2,1,0:T(8,128)(2,1)} %k_in.1, bf16[1,128,4096]{2,1,0:T(8,128)(2,1)} %v_in.1, bf16[1,128,4096]{2,1,0:T(8,128)(2,1)} %g_in.1), custom_call_target="tpu_custom_call" | custom-call | flops 4294967296 | bytes 8388608 | tf_op jit(solution)/shard_map/pallas_call | solution.py:369
  68.5 1.0 %copy.10 = bf16[1,512,1024]{2,1,0:T(8,128)(2,1)} copy(bf16[1,512,1024]{2,1,0:T(8,128)(2,1)S(1)} %get-tuple-element.3) | data formatting | bytes 2097152
  69.4 1.0 %copy.11 = bf16[1,512,1024]{2,1,0:T(8,128)(2,1)} copy(bf16[1,512,1024]{2,1,0:T(8,128)(2,1)S(1)} %get-tuple-element.4) | data formatting | bytes 2097152
  70.4 1.0 %copy.12 = bf16[1,512,1024]{2,1,0:T(8,128)(2,1)} copy(bf16[1,512,1024]{2,1,0:T(8,128)(2,1)S(1)} %get-tuple-element.5) | data formatting | bytes 2097152

commit v3 on v2

--- a/solution.py
+++ b/solution.py
@@ -16,9 +16,9 @@
 TN = (((0,), (0,)), ((), ()))
 WINDOW = 4
 BEFORE = 1
-EARLY = 3
-AT_SUM, AT_TOTAL, AT_PREFIX = 0, 1, 2
-LAG_TOTAL, LAG_PREFIX, LAG_FINISH = 1, 2, 3
+EARLY = 4
+AT_SUM, AT_TOTAL, AT_PREFIX, AT_SHARE, AT_FINISH = 0, 1, 2, 5, 6
+LAG_TOTAL, LAG_PREFIX, LAG_FINISH = 1, 2, 4
 
 
 def dot(a, b, dims):
@@ -32,7 +32,7 @@
     ear, psend, precv, chip, egat, etot, epre, est, mate,
     rounds, y_send, y_recv, y_loc, a_send, a_recv, b_send, b_recv, c_send, c_recv,
     m_send, m_recv, e_loc, e_send, e_recv, p_send, p_recv,
-    ea_send, ea_recv, eb_send, eb_recv, ec_send, ec_recv,
+    ea_send, ea_recv, eb_send, eb_recv, ec_send, ec_recv, ed_send, ed_recv,
 ):
     ny = lax.axis_size("head")
     y = lax.axis_index("head")
@@ -64,17 +64,28 @@
         return {"ctx": lax.rem(x + d, nx) * row + me}
 
     partner = place(x, z, 1 - core)
-    z_next = [place(x, lax.rem(z + d, nz), core) for d in (1, nz - 1)]
-    x_next = [x_peer(d) for d in (1, nx - 1)]
-    near = [y_peer(d) for d in dists] + [partner] + z_next + x_next
+    near = [y_peer(d) for d in dists] + [partner] + [x_peer(d) for d in (1, nx - 1)]
 
     def signal(sem, device):
         pl.semaphore_signal(sem, inc=1, device_id=device, device_id_type=MESH)
+
+    def signal_line(sem, step):
+        @pl.when(z >= step)
+        def _():
+            signal(sem, place(x, z - step, core))
+
+        @pl.when(z + step < nz)
+        def _():
+            signal(sem, place(x, z + step, core))
+
+    def line_count(step):
+        return lax.min(z // step, 1) + lax.min((nz - 1 - z) // step, 1)
 
     barrier = pltpu.get_barrier_semaphore()
     for device in near:
         signal(barrier, device)
-    pl.semaphore_wait(barrier, len(near))
+    signal_line(barrier, 1)
+    pl.semaphore_wait(barrier, len(near) + line_count(1))
 
     def remote(src, dst, send, recv, device):
         pltpu.make_async_remote_copy(
@@ -174,11 +185,14 @@
             at = s + core * (nz - 1 - 2 * s)
             epre[at] = run
             run = run + egat[at]
-        mine = core * nz + z
-        for d in range(1, row):
-            t, peer = row_peer(d)
-            remote(epre.at[t // 2], est.at[mine], ec_send, ec_recv, peer)
-        est[mine] = epre[z]
+        for d in range(1, nz):
+            t = lax.rem(z + d, nz)
+            remote(epre.at[t], est.at[core, z], ec_send, ec_recv, place(x, t, core))
+        est[core, z] = epre[z]
+
+    def early_share():
+        wait_bytes(est.at[0, 0 : nz - 1], ec_recv)
+        remote(est.at[core], est.at[core], ed_send, ed_recv, partner)
 
     def wait_y(h):
         wait_bytes(xin.at[h, 0 : ny - 1], y_recv.at[h])
@@ -266,21 +280,22 @@
         e = h - normal
         wait_bytes(mate.at[0, e], m_recv.at[e])
         late = mate[1, e]
-        ks = est[0:nz, e].reshape(HD, HD) + jnp.where(core == 1, late, 0.0)
-        qs = est[nz : 2 * nz, e].reshape(HD, HD) + jnp.where(core == 0, late, 0.0)
+        ks = est[0, :, e].reshape(HD, HD) + jnp.where(core == 1, late, 0.0)
+        qs = est[1, :, e].reshape(HD, HD) + jnp.where(core == 0, late, 0.0)
         finish(h, ks.astype(jnp.bfloat16), qs.astype(jnp.bfloat16))
 
     for h in range(min(WINDOW, BEFORE)):
         send_y(h)
     early_rows()
     for r in range(rounds.shape[0]):
-        for device in z_next + x_next:
-            signal(rounds.at[r], device)
+        signal_line(rounds.at[r], 2**r)
         if r == 0:
+            for d in (1, nx - 1):
+                signal(rounds.at[r], x_peer(d))
             early_parts()
             for h in range(BEFORE, min(WINDOW, heads)):
                 send_y(h)
-        pl.semaphore_wait(rounds.at[r], 4)
+        pl.semaphore_wait(rounds.at[r], line_count(2**r) + (2 if r == 0 else 0))
 
     @pl.loop(0, heads)
     def _(h):
@@ -297,37 +312,37 @@
         @pl.when(h >= normal)
         def _():
             late_state(h)
-
-        @pl.when(h == AT_SUM)
-        def _():
-            early_sum()
-
-        causal(h)
 
         def lagged(lag, first, end, fn):
             @pl.when((h - lag >= first) & (h - lag < end))
             def _():
                 fn(h - lag)
 
+        def at(step, fn):
+            @pl.when(h == step)
+            def _():
+                fn()
+
+        at(AT_SUM, early_sum)
+        lagged(LAG_PREFIX, 0, normal, prefixes)
+        causal(h)
         lagged(LAG_TOTAL, 0, normal, totals)
-
-        @pl.when(h == AT_TOTAL)
-        def _():
-            early_totals()
-
-        lagged(LAG_PREFIX, 0, normal, prefixes)
-
-        @pl.when(h == AT_PREFIX)
-        def _():
-            early_prefixes()
-
+        at(AT_TOTAL, early_totals)
+        at(AT_PREFIX, early_prefixes)
         lagged(LAG_FINISH, 0, normal, finish_normal)
-
-        @pl.when(h == normal)
-        def _():
-            wait_bytes(est.at[0 : row - 1], ec_recv)
-
-        lagged(1, normal, heads, finish_early)
+        at(AT_SHARE, early_share)
+
+        @pl.when(h == AT_FINISH)
+        def _():
+            wait_bytes(est.at[0], ed_recv)
+
+            @pl.loop(normal, AT_FINISH)
+            def _(g):
+                finish_early(g)
+
+        @pl.when(h > AT_FINISH)
+        def _():
+            finish_early(h - 1)
 
     finish_early(heads - 1)
 
@@ -335,7 +350,8 @@
     wait_bytes(precv.at[0 : ny - 1], p_send)
     wait_bytes(egat.at[0 : nz - 1], ea_send)
     wait_bytes(etot.at[0 : nx - 1], eb_send)
-    wait_bytes(est.at[0 : row - 1], ec_send)
+    wait_bytes(est.at[0, 0 : nz - 1], ec_send)
+    wait_bytes(est.at[0], ed_send)
 
     @pl.loop(0, heads)
     def _(h):
@@ -386,14 +402,14 @@
             pltpu.VMEM((nz, early, per, HD), f32),
             pltpu.VMEM((nx, early, per, HD), f32),
             pltpu.VMEM((nz, early, per, HD), f32),
-            pltpu.VMEM((row, early, per, HD), f32),
+            pltpu.VMEM((2, nz, early, per, HD), f32),
             pltpu.VMEM((2, early, HD, HD), f32),
-            pltpu.SemaphoreType.REGULAR((nz // 2,)),
+            pltpu.SemaphoreType.REGULAR(((nz - 1).bit_length(),)),
         ]
         + [dma((heads,))] * 3
         + [dma((normal,))] * 6
         + [dma((early,))] * 2
-        + [dma] * 11,
+        + [dma] * 13,
         compiler_params=pltpu.CompilerParams(
             collective_id=1, has_side_effects=True, vmem_limit_bytes=44 * 2**20
         ),

time: 71.5 us -> 64.7 us (0.905)
  Pallas kernels: 67.8 us -> 61 us
    pallas_call x1, Pallas kernels: 67.8 us -> 61 us  [shards(): pl.pallas_call(functools.partial(kernel, heads, nx, row, factor), out_sha...]
where the time goes in v3:
time: 64.7 us; the launch traced here: 64.6 us
  Pallas kernels  61 us (94%)
  local copies, waits for them, and re-layouts  2.91 us (4%)
    pallas_call x1, Pallas kernels, shards(): pl.pallas_call(functools.partial(kernel, heads, nx, row, factor), out_sha...  61 us
    unnamed x3, local copies, waits for them, and re-layouts  2.91 us

profile of v3, /device:TPU:1, one launch (start us, length us, event | category | flops | bytes accessed | tf_op | source)
XLA Modules:
  0.0 64.6 jit_solution(12533553469687056453)
XLA Ops:
  0.6 61.0 %shard_map.67 = (bf16[1,512,1024]{2,1,0:T(8,128)(2,1)S(1)}, bf16[1,512,1024]{2,1,0:T(8,128)(2,1)S(1)}, bf16[1,512,1024]{2,1,0:T(8,128)(2,1)S(1)}) custom-call(bf16[1,128,4096]{2,1,0:T(8,128)(2,1)} %q_in.1, bf16[1,128,4096]{2,1,0:T(8,128)(2,1)} %k_in.1, bf16[1,128,4096]{2,1,0:T(8,128)(2,1)} %v_in.1, bf16[1,128,4096]{2,1,0:T(8,128)(2,1)} %g_in.1), custom_call_target="tpu_custom_call" | custom-call | flops 4294967296 | bytes 8388608 | tf_op jit(solution)/shard_map/pallas_call | solution.py:385
  61.7 1.0 %copy.10 = bf16[1,512,1024]{2,1,0:T(8,128)(2,1)} copy(bf16[1,512,1024]{2,1,0:T(8,128)(2,1)S(1)} %get-tuple-element.3) | data formatting | bytes 2097152
  62.7 1.0 %copy.11 = bf16[1,512,1024]{2,1,0:T(8,128)(2,1)} copy(bf16[1,512,1024]{2,1,0:T(8,128)(2,1)S(1)} %get-tuple-element.4) | data formatting | bytes 2097152
  63.6 1.0 %copy.12 = bf16[1,512,1024]{2,1,0:T(8,128)(2,1)} copy(bf16[1,512,1024]{2,1,0:T(8,128)(2,1)S(1)} %get-tuple-element.5) | data formatting | bytes 2097152

commit v4 on v3

--- a/solution.py
+++ b/solution.py
@@ -16,8 +16,11 @@
 TN = (((0,), (0,)), ((), ()))
 WINDOW = 4
 BEFORE = 1
+AHEAD = 0
+BUSY = 3
+PIECES = 2
 EARLY = 4
-AT_SUM, AT_TOTAL, AT_PREFIX, AT_SHARE, AT_FINISH = 0, 1, 2, 5, 6
+AT_SUM, AT_TOTAL, AT_PREFIX, AT_SHARE, AT_FINISH = 1, 2, 3, 5, 6
 LAG_TOTAL, LAG_PREFIX, LAG_FINISH = 1, 2, 4
 
 
@@ -50,6 +53,10 @@
     normal = heads - early
     dists = (2, 1, 3)
 
+    row_order = sorted(range(1, row), key=lambda d: -min(d, row - d))
+    z_order = sorted(range(1, nz), key=lambda d: -min(d, nz - d))
+    x_order = sorted(range(1, nx), key=lambda d: -min(d, nx - d))
+
     def y_peer(d):
         return {"head": lax.rem(y + d, ny)}
 
@@ -102,15 +109,15 @@
     def cols(owner, h, count=1):
         return pl.ds(pl.multiple_of((owner * heads + h) * HD, HD), count * HD)
 
-    def send_y(h):
+    def send_y(h, arrays=range(4), local=True):
         for d in dists:
             tgt = lax.rem(y + d, ny)
-            for a in range(4):
+            for a in arrays:
                 remote(
                     ins[a].at[0, :, cols(tgt, h)], xin.at[h, a, my_rows(y), :],
                     y_send.at[h], y_recv.at[h], {"head": tgt},
                 )
-        for a in range(4):
+        for a in range(4 if local else 0):
             pltpu.make_async_copy(
                 ins[a].at[0, :, cols(y, h)], xin.at[h, a, my_rows(y), :], y_loc.at[h]
             ).start()
@@ -158,7 +165,7 @@
                 got = precv[lax.rem(y + d, ny), e].astype(jnp.float32)
                 total = total + got.reshape(nz, per, HD)
             chip[:, e] = total
-        for d in range(1, nz):
+        for d in z_order:
             t = lax.rem(z + d, nz)
             remote(chip.at[t], egat.at[z], ea_send, ea_recv, place(x, t, core))
         egat[z] = chip[z]
@@ -169,7 +176,7 @@
         for s in range(1, nz):
             total = total + egat[s]
         etot[x] = total
-        for d in range(1, nx):
+        for d in x_order:
             remote(etot.at[x], etot.at[x], eb_send, eb_recv, x_peer(d))
 
     def base(parts, x_side):
@@ -185,7 +192,7 @@
             at = s + core * (nz - 1 - 2 * s)
             epre[at] = run
             run = run + egat[at]
-        for d in range(1, nz):
+        for d in z_order:
             t = lax.rem(z + d, nz)
             remote(epre.at[t], est.at[core, z], ec_send, ec_recv, place(x, t, core))
         est[core, z] = epre[z]
@@ -201,7 +208,7 @@
     def states(h):
         own[h, 0:HD, :] = dot(xin[h, 1], xin[h, 2], TN)
         own[h, HD : 2 * HD, :] = dot(xin[h, 0], xin[h, 3], TN)
-        for d in range(1, row):
+        for d in row_order:
             t, peer = row_peer(d)
             src = own.at[h, pl.ds(pl.multiple_of(t * per, per), per), :]
             remote(src, gat.at[h, me], a_send.at[h], a_recv.at[h], peer)
@@ -218,7 +225,7 @@
         for s in range(1, row):
             total = total + gat[h, s]
         tot[h, x] = total
-        for d in range(1, nx):
+        for d in x_order:
             remote(tot.at[h, x], tot.at[h, x], b_send.at[h], b_recv.at[h], x_peer(d))
 
     def prefixes(h):
@@ -228,7 +235,7 @@
             at = s + is_q * (row - 1 - 2 * s)
             pre[h, at] = run.astype(jnp.bfloat16)
             run = run + gat[h, at]
-        for d in range(1, row):
+        for d in row_order:
             t, peer = row_peer(d)
             remote(pre.at[h, t], st.at[h, me], c_send.at[h], c_recv.at[h], peer)
         st[h, me] = pre[h, me]
@@ -287,13 +294,16 @@
     for h in range(min(WINDOW, BEFORE)):
         send_y(h)
     early_rows()
+    if AHEAD:
+        send_y(BEFORE, range(AHEAD), False)
     for r in range(rounds.shape[0]):
         signal_line(rounds.at[r], 2**r)
         if r == 0:
             for d in (1, nx - 1):
                 signal(rounds.at[r], x_peer(d))
             early_parts()
-            for h in range(BEFORE, min(WINDOW, heads)):
+            send_y(BEFORE, range(AHEAD, 4))
+            for h in range(BEFORE + 1, min(WINDOW, heads)):
                 send_y(h)
         pl.semaphore_wait(rounds.at[r], line_count(2**r) + (2 if r == 0 else 0))
 
@@ -325,8 +335,9 @@
 
         at(AT_SUM, early_sum)
         lagged(LAG_PREFIX, 0, normal, prefixes)
+        lagged(LAG_TOTAL, BUSY, normal, totals)
         causal(h)
-        lagged(LAG_TOTAL, 0, normal, totals)
+        lagged(LAG_TOTAL, 0, BUSY, totals)
         at(AT_TOTAL, early_totals)
         at(AT_PREFIX, early_prefixes)
         lagged(LAG_FINISH, 0, normal, finish_normal)
@@ -336,15 +347,13 @@
         def _():
             wait_bytes(est.at[0], ed_recv)
 
-            @pl.loop(normal, AT_FINISH)
+            @pl.loop(normal, AT_FINISH + 1)
             def _(g):
                 finish_early(g)
 
         @pl.when(h > AT_FINISH)
         def _():
-            finish_early(h - 1)
-
-    finish_early(heads - 1)
+            finish_early(h)
 
     wait_bytes(ear.at[0], e_send)
     wait_bytes(precv.at[0 : ny - 1], p_send)
@@ -366,6 +375,19 @@
     @pl.loop(0, early)
     def _(e):
         wait_bytes(mate.at[0, e], m_send.at[e])
+
+
+def store(gq_in, gk_in, gv_in, gq_out, gk_out, gv_out, sems):
+    pairs = ((gq_in, gq_out), (gk_in, gk_out), (gv_in, gv_out))
+    copies = []
+    for i, (src, dst) in enumerate(pairs):
+        for j in range(sems.shape[1]):
+            at = pl.ds(j * (BLOCK // sems.shape[1]), BLOCK // sems.shape[1])
+            copies.append(pltpu.make_async_copy(src.at[0, at, :], dst.at[0, at, :], sems.at[i, j]))
+    for copy in copies:
+        copy.start()
+    for copy in copies:
+        copy.wait()
 
 
 def shards(nx, query, keys, values, grad_out):
@@ -382,7 +404,7 @@
     flops = heads * (9 * 2 * BLOCK * BLOCK * HD * 3 // 4 + 5 * 2 * BLOCK * HD * HD)
     ins = [pltpu.with_memory_space_constraint(a, pltpu.HBM) for a in (query, keys, values, grad_out)]
     f32, bf16 = jnp.float32, jnp.bfloat16
-    return pl.pallas_call(
+    grads = pl.pallas_call(
         functools.partial(kernel, heads, nx, row, factor),
         out_shape=[pltpu.VMEM((1, BLOCK, heads * HD), bf16)] * 3,
         in_specs=[pl.BlockSpec(memory_space=pltpu.HBM)] * 4,
@@ -415,6 +437,13 @@
         ),
         cost_estimate=pl.CostEstimate(flops=flops, bytes_accessed=8 * 2**20, transcendentals=0),
     )(*ins)
+    return pl.pallas_call(
+        store,
+        out_shape=[jax.ShapeDtypeStruct(a.shape, a.dtype) for a in grads],
+        in_specs=[pl.BlockSpec(memory_space=pltpu.VMEM)] * 3,
+        out_specs=[pl.BlockSpec(memory_space=pltpu.HBM)] * 3,
+        scratch_shapes=[dma((3, PIECES))],
+    )(*[pltpu.with_memory_space_constraint(a, pltpu.VMEM) for a in grads])
 
 
 def solution(mesh):

time: 64.7 us -> 63.2 us (0.977)
  local copies, waits for them, and re-layouts: 2.91 us -> 0 us
  Pallas kernels: 61 us -> 62.5 us
    unnamed x3 -> x0, local copies, waits for them, and re-layouts: 2.91 us -> none
    pallas_call x0 -> x1, Pallas kernels: none -> 1.71 us  [shards(): pl.pallas_call(store, out_shape=[jax.ShapeDtypeStruct(a.shape, a.dtype) f...]
where the time goes in v4:
time: 63.2 us; the launch traced here: 63.1 us
  Pallas kernels  62.5 us (99%)
  between operations  0.64 us (1%)
    pallas_call x1, Pallas kernels, shards(): pl.pallas_call(functools.partial(kernel, heads, nx, row, factor), out_sha...  60.8 us
    pallas_call x1, Pallas kernels, shards(): pl.pallas_call(store, out_shape=[jax.ShapeDtypeStruct(a.shape, a.dtype) f...  1.71 us

profile of v4, /device:TPU:1, one launch (start us, length us, event | category | flops | bytes accessed | tf_op | source)
XLA Modules:
  0.0 63.1 jit_solution(6068795833099900209)
XLA Ops:
  0.6 60.8 %shard_map.67 = (bf16[1,512,1024]{2,1,0:T(8,128)(2,1)S(1)}, bf16[1,512,1024]{2,1,0:T(8,128)(2,1)S(1)}, bf16[1,512,1024]{2,1,0:T(8,128)(2,1)S(1)}) custom-call(bf16[1,128,4096]{2,1,0:T(8,128)(2,1)} %q_in.1, bf16[1,128,4096]{2,1,0:T(8,128)(2,1)} %k_in.1, bf16[1,128,4096]{2,1,0:T(8,128)(2,1)} %v_in.1, bf16[1,128,4096]{2,1,0:T(8,128)(2,1)} %g_in.1), custom_call_target="tpu_custom_call" | custom-call | flops 4294967296 | bytes 8388608 | tf_op jit(solution)/shard_map/pallas_call | solution.py:407
  61.4 1.7 %shard_map.68 = (bf16[1,512,1024]{2,1,0:T(8,128)(2,1)}, bf16[1,512,1024]{2,1,0:T(8,128)(2,1)}, bf16[1,512,1024]{2,1,0:T(8,128)(2,1)}) custom-call(bf16[1,512,1024]{2,1,0:T(8,128)(2,1)S(1)} %get-tuple-element.6.gq_in, bf16[1,512,1024]{2,1,0:T(8,128)(2,1)S(1)} %get-tuple-element.7.gk_in, bf16[1,512,1024]{2,1,0:T(8,128)(2,1)S(1)} %get-tuple-element.8.gv_in), custom_call_target="tpu_custom_call" | custom-call | tf_op jit(solution)/shard_map/pallas_call | solution.py:440

commit v5 on v4

--- a/solution.py
+++ b/solution.py
@@ -14,9 +14,9 @@
 NT = (((1,), (1,)), ((), ()))
 NN = (((1,), (0,)), ((), ()))
 TN = (((0,), (0,)), ((), ()))
-WINDOW = 4
+WINDOW = 5
 BEFORE = 1
-AHEAD = 0
+BETWEEN = 2
 BUSY = 3
 PIECES = 2
 EARLY = 4
@@ -32,9 +32,9 @@
     heads, nx, row, factor,
     q_in, k_in, v_in, g_in, gq_out, gk_out, gv_out,
     xin, acc, own, gat, tot, pre, st,
-    ear, psend, precv, chip, egat, etot, epre, est, mate,
+    ear, psend, pkeep, phop, precv, chip, egat, etot, epre, est, mate,
     rounds, y_send, y_recv, y_loc, a_send, a_recv, b_send, b_recv, c_send, c_recv,
-    m_send, m_recv, e_loc, e_send, e_recv, p_send, p_recv,
+    m_send, m_recv, e_loc, e_send, e_recv, h_send, h_recv, p_send, p_recv,
     ea_send, ea_recv, eb_send, eb_recv, ec_send, ec_recv, ed_send, ed_recv,
 ):
     ny = lax.axis_size("head")
@@ -109,15 +109,15 @@
     def cols(owner, h, count=1):
         return pl.ds(pl.multiple_of((owner * heads + h) * HD, HD), count * HD)
 
-    def send_y(h, arrays=range(4), local=True):
+    def send_y(h):
         for d in dists:
             tgt = lax.rem(y + d, ny)
-            for a in arrays:
+            for a in range(4):
                 remote(
                     ins[a].at[0, :, cols(tgt, h)], xin.at[h, a, my_rows(y), :],
                     y_send.at[h], y_recv.at[h], {"head": tgt},
                 )
-        for a in range(4 if local else 0):
+        for a in range(4):
             pltpu.make_async_copy(
                 ins[a].at[0, :, cols(y, h)], xin.at[h, a, my_rows(y), :], y_loc.at[h]
             ).start()
@@ -145,26 +145,47 @@
     def early_parts():
         wait_bytes(ear.at[0], e_loc)
         wait_bytes(ear.at[0], e_recv)
+        top, low = slice(0, HD // 2), slice(HD // 2, HD)
         for d in (2, 1, 3, 0):
             t = lax.rem(y + d, ny)
             for e in range(early):
                 at = slice(e * HD, (e + 1) * HD)
                 part = dot(ear[0, t, :, at], ear[1, t, :, at], TN)
-                if d:
-                    psend[d, e] = part.astype(jnp.bfloat16)
+                if d == 0:
+                    chip[:, e] = part.reshape(nz, per, HD)
+                elif d == 2:
+                    psend[0, e] = part[top].astype(jnp.bfloat16)
+                    psend[1, e] = part[low].astype(jnp.bfloat16)
+                elif d == 1:
+                    psend[2, e] = part[top].astype(jnp.bfloat16)
+                    pkeep[0, e] = part[low]
                 else:
-                    chip[:, e] = part.reshape(nz, per, HD)
-            if d:
-                remote(psend.at[d], precv.at[y], p_send, p_recv, y_peer(d))
+                    psend[3, e] = part[low].astype(jnp.bfloat16)
+                    pkeep[1, e] = part[top]
+            if d == 2:
+                remote(psend.at[0], phop.at[0], h_send, h_recv, y_peer(ny - 1))
+                remote(psend.at[1], phop.at[1], h_send, h_recv, y_peer(1))
+            elif d == 1:
+                remote(psend.at[2], precv.at[0, 0], p_send, p_recv, y_peer(1))
+            elif d == 3:
+                remote(psend.at[3], precv.at[1, 1], p_send, p_recv, y_peer(ny - 1))
+
+    def early_merge():
+        wait_bytes(phop, h_recv)
+        for e in range(early):
+            psend[4, e] = (pkeep[0, e] + phop[1, e].astype(jnp.float32)).astype(jnp.bfloat16)
+            psend[5, e] = (pkeep[1, e] + phop[0, e].astype(jnp.float32)).astype(jnp.bfloat16)
+        remote(psend.at[4], precv.at[0, 1], p_send, p_recv, y_peer(1))
+        remote(psend.at[5], precv.at[1, 0], p_send, p_recv, y_peer(ny - 1))
 
     def early_sum():
-        wait_bytes(precv.at[0 : ny - 1], p_recv)
+        wait_bytes(precv, p_recv)
+        half = nz // 2
         for e in range(early):
-            total = chip[:, e]
-            for d in range(1, ny):
-                got = precv[lax.rem(y + d, ny), e].astype(jnp.float32)
-                total = total + got.reshape(nz, per, HD)
-            chip[:, e] = total
+            for i in range(2):
+                at = slice(i * half, (i + 1) * half)
+                got = precv[0, i, e].astype(jnp.float32) + precv[1, i, e].astype(jnp.float32)
+                chip[at, e] = chip[at, e] + got.reshape(half, per, HD)
         for d in z_order:
             t = lax.rem(z + d, nz)
             remote(chip.at[t], egat.at[z], ea_send, ea_recv, place(x, t, core))
@@ -291,21 +312,27 @@
         qs = est[1, :, e].reshape(HD, HD) + jnp.where(core == 0, late, 0.0)
         finish(h, ks.astype(jnp.bfloat16), qs.astype(jnp.bfloat16))
 
-    for h in range(min(WINDOW, BEFORE)):
+    def wait_round(r):
+        pl.semaphore_wait(rounds.at[r], line_count(2**r) + (2 if r == 0 else 0))
+
+    for h in range(BEFORE):
         send_y(h)
     early_rows()
-    if AHEAD:
-        send_y(BEFORE, range(AHEAD), False)
-    for r in range(rounds.shape[0]):
-        signal_line(rounds.at[r], 2**r)
-        if r == 0:
-            for d in (1, nx - 1):
-                signal(rounds.at[r], x_peer(d))
-            early_parts()
-            send_y(BEFORE, range(AHEAD, 4))
-            for h in range(BEFORE + 1, min(WINDOW, heads)):
-                send_y(h)
-        pl.semaphore_wait(rounds.at[r], line_count(2**r) + (2 if r == 0 else 0))
+    signal_line(rounds.at[0], 1)
+    for d in (1, nx - 1):
+        signal(rounds.at[0], x_peer(d))
+    early_parts()
+    for h in range(BEFORE, BETWEEN):
+        send_y(h)
+    wait_round(0)
+    signal_line(rounds.at[1], 2)
+    early_merge()
+    for h in range(BETWEEN, min(WINDOW, heads)):
+        send_y(h)
+    for r in range(1, rounds.shape[0]):
+        wait_round(r)
+        if r + 1 < rounds.shape[0]:
+            signal_line(rounds.at[r + 1], 2 ** (r + 1))
 
     @pl.loop(0, heads)
     def _(h):
@@ -356,7 +383,8 @@
             finish_early(h)
 
     wait_bytes(ear.at[0], e_send)
-    wait_bytes(precv.at[0 : ny - 1], p_send)
+    wait_bytes(phop, h_send)
+    wait_bytes(precv, p_send)
     wait_bytes(egat.at[0 : nz - 1], ea_send)
     wait_bytes(etot.at[0 : nx - 1], eb_send)
     wait_bytes(est.at[0, 0 : nz - 1], ec_send)
@@ -418,8 +446,10 @@
             pltpu.VMEM((normal, row, per, HD), bf16),
             pltpu.VMEM((normal, row, per, HD), bf16),
             pltpu.VMEM((2, ny, 2 * BLOCK // ny, early * HD), bf16),
-            pltpu.VMEM((ny, early, HD, HD), bf16),
-            pltpu.VMEM((ny, early, HD, HD), bf16),
+            pltpu.VMEM((6, early, HD // 2, HD), bf16),
+            pltpu.VMEM((2, early, HD // 2, HD), f32),
+            pltpu.VMEM((2, early, HD // 2, HD), bf16),
+            pltpu.VMEM((2, 2, early, HD // 2, HD), bf16),
             pltpu.VMEM((nz, early, per, HD), f32),
             pltpu.VMEM((nz, early, per, HD), f32),
             pltpu.VMEM((nx, early, per, HD), f32),
@@ -431,7 +461,7 @@
         + [dma((heads,))] * 3
         + [dma((normal,))] * 6
         + [dma((early,))] * 2
-        + [dma] * 13,
+        + [dma] * 15,
         compiler_params=pltpu.CompilerParams(
             collective_id=1, has_side_effects=True, vmem_limit_bytes=44 * 2**20
         ),

time: 63.2 us -> 61.8 us (0.978)
  Pallas kernels: 62.5 us -> 61 us
    pallas_call x1, Pallas kernels: 60.8 us -> 59.3 us  [shards(): pl.pallas_call(functools.partial(kernel, heads, nx, row, factor), out_sha...]
where the time goes in v5:
time: 61.8 us; the launch traced here: 61.7 us
  Pallas kernels  61 us (99%)
  between operations  0.64 us (1%)
    pallas_call x1, Pallas kernels, shards(): pl.pallas_call(functools.partial(kernel, heads, nx, row, factor), out_sha...  59.3 us
    pallas_call x1, Pallas kernels, shards(): pl.pallas_call(store, out_shape=[jax.ShapeDtypeStruct(a.shape, a.dtype) f...  1.71 us

profile of v5, /device:TPU:1, one launch (start us, length us, event | category | flops | bytes accessed | tf_op | source)
XLA Modules:
  0.0 61.7 jit_solution(5714332327734060939)
XLA Ops:
  0.6 59.3 %shard_map.67 = (bf16[1,512,1024]{2,1,0:T(8,128)(2,1)S(1)}, bf16[1,512,1024]{2,1,0:T(8,128)(2,1)S(1)}, bf16[1,512,1024]{2,1,0:T(8,128)(2,1)S(1)}) custom-call(bf16[1,128,4096]{2,1,0:T(8,128)(2,1)} %q_in.1, bf16[1,128,4096]{2,1,0:T(8,128)(2,1)} %k_in.1, bf16[1,128,4096]{2,1,0:T(8,128)(2,1)} %v_in.1, bf16[1,128,4096]{2,1,0:T(8,128)(2,1)} %g_in.1), custom_call_target="tpu_custom_call" | custom-call | flops 4294967296 | bytes 8388608 | tf_op jit(solution)/shard_map/pallas_call | solution.py:435
  59.9 1.7 %shard_map.68 = (bf16[1,512,1024]{2,1,0:T(8,128)(2,1)}, bf16[1,512,1024]{2,1,0:T(8,128)(2,1)}, bf16[1,512,1024]{2,1,0:T(8,128)(2,1)}) custom-call(bf16[1,512,1024]{2,1,0:T(8,128)(2,1)S(1)} %get-tuple-element.6.gq_in, bf16[1,512,1024]{2,1,0:T(8,128)(2,1)S(1)} %get-tuple-element.7.gk_in, bf16[1,512,1024]{2,1,0:T(8,128)(2,1)S(1)} %get-tuple-element.8.gv_in), custom_call_target="tpu_custom_call" | custom-call | tf_op jit(solution)/shard_map/pallas_call | solution.py:470

commit v6 on v5

--- a/solution.py
+++ b/solution.py
@@ -14,7 +14,7 @@
 NT = (((1,), (1,)), ((), ()))
 NN = (((1,), (0,)), ((), ()))
 TN = (((0,), (0,)), ((), ()))
-WINDOW = 5
+WINDOW = 6
 BEFORE = 1
 BETWEEN = 2
 BUSY = 3
@@ -33,7 +33,7 @@
     q_in, k_in, v_in, g_in, gq_out, gk_out, gv_out,
     xin, acc, own, gat, tot, pre, st,
     ear, psend, pkeep, phop, precv, chip, egat, etot, epre, est, mate,
-    rounds, y_send, y_recv, y_loc, a_send, a_recv, b_send, b_recv, c_send, c_recv,
+    rounds, reply, y_send, y_recv, y_loc, a_send, a_recv, b_send, b_recv, c_send, c_recv,
     m_send, m_recv, e_loc, e_send, e_recv, h_send, h_recv, p_send, p_recv,
     ea_send, ea_recv, eb_send, eb_recv, ec_send, ec_recv, ed_send, ed_recv,
 ):
@@ -71,7 +71,6 @@
         return {"ctx": lax.rem(x + d, nx) * row + me}
 
     partner = place(x, z, 1 - core)
-    near = [y_peer(d) for d in dists] + [partner] + [x_peer(d) for d in (1, nx - 1)]
 
     def signal(sem, device):
         pl.semaphore_signal(sem, inc=1, device_id=device, device_id_type=MESH)
@@ -85,14 +84,48 @@
         def _():
             signal(sem, place(x, z + step, core))
 
+        if step < nx:
+            @pl.when(x >= step)
+            def _():
+                signal(sem, place(x - step, z, core))
+
+            @pl.when(x + step < nx)
+            def _():
+                signal(sem, place(x + step, z, core))
+
     def line_count(step):
-        return lax.min(z // step, 1) + lax.min((nz - 1 - z) // step, 1)
+        count = lax.min(z // step, 1) + lax.min((nz - 1 - z) // step, 1)
+        return count + lax.min(x // step, 1) + lax.min((nx - 1 - x) // step, 1)
 
     barrier = pltpu.get_barrier_semaphore()
-    for device in near:
-        signal(barrier, device)
-    signal_line(barrier, 1)
-    pl.semaphore_wait(barrier, len(near) + line_count(1))
+    for d in dists:
+        signal(barrier, y_peer(d))
+
+    @pl.when(core == 1)
+    def _():
+        signal(barrier, partner)
+
+    @pl.when(z + 1 < nz)
+    def _():
+        signal(barrier, place(x, z + 1, core))
+
+    @pl.when(x + 1 < nx)
+    def _():
+        signal(barrier, place(x + 1, z, core))
+
+    pl.semaphore_wait(barrier, ny - 1 + (1 - core) + lax.min(z, 1) + lax.min(x, 1))
+
+    @pl.when(core == 0)
+    def _():
+        signal(reply.at[0], partner)
+
+    @pl.when(z >= 1)
+    def _():
+        signal(reply.at[1], place(x, z - 1, core))
+
+    @pl.when(x >= 1)
+    def _():
+        signal(reply.at[2], place(x - 1, z, core))
 
     def remote(src, dst, send, recv, device):
         pltpu.make_async_remote_copy(
@@ -313,23 +346,33 @@
         finish(h, ks.astype(jnp.bfloat16), qs.astype(jnp.bfloat16))
 
     def wait_round(r):
-        pl.semaphore_wait(rounds.at[r], line_count(2**r) + (2 if r == 0 else 0))
+        pl.semaphore_wait(rounds.at[r], line_count(2**r))
 
     for h in range(BEFORE):
         send_y(h)
+
+    @pl.when(core == 1)
+    def _():
+        pl.semaphore_wait(reply.at[0], 1)
+
     early_rows()
-    signal_line(rounds.at[0], 1)
-    for d in (1, nx - 1):
-        signal(rounds.at[0], x_peer(d))
     early_parts()
     for h in range(BEFORE, BETWEEN):
         send_y(h)
-    wait_round(0)
-    signal_line(rounds.at[1], 2)
+
+    @pl.when(z + 1 < nz)
+    def _():
+        pl.semaphore_wait(reply.at[1], 1)
+
+    @pl.when(x + 1 < nx)
+    def _():
+        pl.semaphore_wait(reply.at[2], 1)
+
+    signal_line(rounds.at[0], 1)
     early_merge()
     for h in range(BETWEEN, min(WINDOW, heads)):
         send_y(h)
-    for r in range(1, rounds.shape[0]):
+    for r in range(rounds.shape[0]):
         wait_round(r)
         if r + 1 < rounds.shape[0]:
             signal_line(rounds.at[r + 1], 2 ** (r + 1))
@@ -457,6 +500,7 @@
             pltpu.VMEM((2, nz, early, per, HD), f32),
             pltpu.VMEM((2, early, HD, HD), f32),
             pltpu.SemaphoreType.REGULAR(((nz - 1).bit_length(),)),
+            pltpu.SemaphoreType.REGULAR((3,)),
         ]
         + [dma((heads,))] * 3
         + [dma((normal,))] * 6

time: 61.8 us -> 60.2 us (0.974)
  Pallas kernels: 61 us -> 59.5 us
    pallas_call x1, Pallas kernels: 59.3 us -> 57.8 us  [shards(): pl.pallas_call(functools.partial(kernel, heads, nx, row, factor), out_sha...]
where the time goes in v6:
time: 60.2 us; the launch traced here: 60.1 us
  Pallas kernels  59.5 us (99%)
  between operations  0.64 us (1%)
    pallas_call x1, Pallas kernels, shards(): pl.pallas_call(functools.partial(kernel, heads, nx, row, factor), out_sha...  57.8 us
    pallas_call x1, Pallas kernels, shards(): pl.pallas_call(store, out_shape=[jax.ShapeDtypeStruct(a.shape, a.dtype) f...  1.71 us

profile of v6, /device:TPU:1, one launch (start us, length us, event | category | flops | bytes accessed | tf_op | source)
XLA Modules:
  0.0 60.1 jit_solution(17744303302263009009)
XLA Ops:
  0.6 57.8 %shard_map.67 = (bf16[1,512,1024]{2,1,0:T(8,128)(2,1)S(1)}, bf16[1,512,1024]{2,1,0:T(8,128)(2,1)S(1)}, bf16[1,512,1024]{2,1,0:T(8,128)(2,1)S(1)}) custom-call(bf16[1,128,4096]{2,1,0:T(8,128)(2,1)} %q_in.1, bf16[1,128,4096]{2,1,0:T(8,128)(2,1)} %k_in.1, bf16[1,128,4096]{2,1,0:T(8,128)(2,1)} %v_in.1, bf16[1,128,4096]{2,1,0:T(8,128)(2,1)} %g_in.1), custom_call_target="tpu_custom_call" | custom-call | flops 4294967296 | bytes 8388608 | tf_op jit(solution)/shard_map/pallas_call | solution.py:478
  58.4 1.7 %shard_map.68 = (bf16[1,512,1024]{2,1,0:T(8,128)(2,1)}, bf16[1,512,1024]{2,1,0:T(8,128)(2,1)}, bf16[1,512,1024]{2,1,0:T(8,128)(2,1)}) custom-call(bf16[1,512,1024]{2,1,0:T(8,128)(2,1)S(1)} %get-tuple-element.6.gq_in, bf16[1,512,1024]{2,1,0:T(8,128)(2,1)S(1)} %get-tuple-element.7.gk_in, bf16[1,512,1024]{2,1,0:T(8,128)(2,1)S(1)} %get-tuple-element.8.gv_in), custom_call_target="tpu_custom_call" | custom-call | tf_op jit(solution)/shard_map/pallas_call | solution.py:514

commit v7 on v6

--- a/solution.py
+++ b/solution.py
@@ -114,18 +114,6 @@
         signal(barrier, place(x + 1, z, core))
 
     pl.semaphore_wait(barrier, ny - 1 + (1 - core) + lax.min(z, 1) + lax.min(x, 1))
-
-    @pl.when(core == 0)
-    def _():
-        signal(reply.at[0], partner)
-
-    @pl.when(z >= 1)
-    def _():
-        signal(reply.at[1], place(x, z - 1, core))
-
-    @pl.when(x >= 1)
-    def _():
-        signal(reply.at[2], place(x - 1, z, core))
 
     def remote(src, dst, send, recv, device):
         pltpu.make_async_remote_copy(
@@ -350,6 +338,18 @@
 
     for h in range(BEFORE):
         send_y(h)
+
+    @pl.when(core == 0)
+    def _():
+        signal(reply.at[0], partner)
+
+    @pl.when(z >= 1)
+    def _():
+        signal(reply.at[1], place(x, z - 1, core))
+
+    @pl.when(x >= 1)
+    def _():
+        signal(reply.at[2], place(x - 1, z, core))
 
     @pl.when(core == 1)
     def _():

time: 60.2 us -> 60.2 us (level)
  no operation moved by 1% of the time
where the time goes in v7:
time: 60.2 us; the launch traced here: 60.1 us
  Pallas kernels  59.5 us (99%)
  between operations  0.64 us (1%)
    pallas_call x1, Pallas kernels, shards(): pl.pallas_call(functools.partial(kernel, heads, nx, row, factor), out_sha...  57.8 us
    pallas_call x1, Pallas kernels, shards(): pl.pallas_call(store, out_shape=[jax.ShapeDtypeStruct(a.shape, a.dtype) f...  1.71 us

profile of v7, /device:TPU:1, one launch (start us, length us, event | category | flops | bytes accessed | tf_op | source)
XLA Modules:
  0.0 60.1 jit_solution(7478729279975417723)
XLA Ops:
  0.6 57.8 %shard_map.67 = (bf16[1,512,1024]{2,1,0:T(8,128)(2,1)S(1)}, bf16[1,512,1024]{2,1,0:T(8,128)(2,1)S(1)}, bf16[1,512,1024]{2,1,0:T(8,128)(2,1)S(1)}) custom-call(bf16[1,128,4096]{2,1,0:T(8,128)(2,1)} %q_in.1, bf16[1,128,4096]{2,1,0:T(8,128)(2,1)} %k_in.1, bf16[1,128,4096]{2,1,0:T(8,128)(2,1)} %v_in.1, bf16[1,128,4096]{2,1,0:T(8,128)(2,1)} %g_in.1), custom_call_target="tpu_custom_call" | custom-call | flops 4294967296 | bytes 8388608 | tf_op jit(solution)/shard_map/pallas_call | solution.py:478
  58.4 1.7 %shard_map.68 = (bf16[1,512,1024]{2,1,0:T(8,128)(2,1)}, bf16[1,512,1024]{2,1,0:T(8,128)(2,1)}, bf16[1,512,1024]{2,1,0:T(8,128)(2,1)}) custom-call(bf16[1,512,1024]{2,1,0:T(8,128)(2,1)S(1)} %get-tuple-element.6.gq_in, bf16[1,512,1024]{2,1,0:T(8,128)(2,1)S(1)} %get-tuple-element.7.gk_in, bf16[1,512,1024]{2,1,0:T(8,128)(2,1)S(1)} %get-tuple-element.8.gv_in), custom_call_target="tpu_custom_call" | custom-call | tf_op jit(solution)/shard_map/pallas_call | solution.py:514
